TPU v7x, 128 devices: a whole 4x4x4 slice. The times are simulated.
128 devices in a mesh: section: 2 (over core), expert: 32 (over z, y, x_lo), dp: 2 (over x_hi).
Axes of the slice: x: 4 (x_hi: 2, x_lo: 2; x = x_hi * 2 + x_lo), y: 4, z: 4, core: 2. Of those that a mesh axis runs over, the one named last changes fastest.
Arguments:
- hidden_held: bfloat16 [2, 4096, 4096], P('section', 'expert'), may hold values from -6 to 6
- fresh_rows: bfloat16 [1, 4096, 4096], P(None, 'expert'), may hold values from -6 to 6
- doc_held: int32 [2, 4096], P('section', 'expert'), may hold values from 0 to 63, never falling along the last dimension, each value on 1 to 128 neighbouring positions
- doc_fresh: int32 [1, 4096], P(None, 'expert'), may hold values from 0 to 63, never falling along the last dimension, each value on 1 to 128 neighbouring positions
- routes: int32 [2, 2, 4096, 2], P(None, 'section', 'expert'), may hold values from 0 to 31, all different within a row; in each aligned block of 128 rows (0 to 127, 128 to 255, ..., all dimensions but the last counted through in order) at most 12 rows name the same one
- attn_gain: bfloat16 [2, 4096], P('section'), may hold values from 0.25 to 1.75
- query_gain: bfloat16 [2, 4096], P('section'), may hold values from -4 to 4
- key_gain: bfloat16 [2, 4096], P('section'), may hold values from -4 to 4
- ffn_gain: bfloat16 [2, 4096], P('section'), may hold values from 0.25 to 1.75
- router: bfloat16 [2, 4096, 32], P('section'), may hold values from -0.09375 to 0.09375
- weight_in: bfloat16 [2, 32, 4096, 2, 1536], P('section', 'expert', None, None, 'dp'), may hold values from -0.09375 to 0.09375
- weight_out: bfloat16 [2, 32, 1536, 4096], P('section', 'expert', 'dp'), may hold values from -0.15625 to 0.15625
Outputs:
- layer_out: bfloat16 [2, 2, 4096, 4096], P(None, 'section', 'expert')
Inputs may be any that keep to these rules, and one draw needn't show every extreme that they name: `doc_held`: ids never fall along a row; every document has at most 128 tokens, and one has exactly 128. `doc_fresh`: ids never fall along a row; every document has at most 128 tokens, and one has exactly 128. `routes`: the 2 experts of a token differ; among the 128 tokens of one device for one step and layer, no expert is chosen more than 12 times, a bound that some block reaches.
All inputs are finite; a program needn't handle non-finite values.
Results may differ from a plain program's by a relative error of at most 0.017.
Values may be sent and summed in bfloat16 or wider, within the bound.
A program may use at most 128 MiB of HBM per device.

v0:
```python
import jax
import jax.numpy as jnp
from jax import lax
from jax.sharding import PartitionSpec as P

HEAD_DIM = 128


def shifted(array, axis, by):
    devices = lax.axis_size(axis)
    pairs = [(i, i + by) for i in range(devices) if 0 <= i + by < devices]
    return lax.ppermute(array, axis, pairs)


def rms_norm(rows, gain):
    wide = rows.astype(jnp.float32)
    return (
        wide
        * lax.rsqrt(jnp.mean(wide * wide, axis=-1, keepdims=True) + 1e-06)
        * gain.astype(jnp.float32)
    )


def attend(own_rows, prior_rows, own_ids, prior_ids, query_gain, key_gain):
    tok_rows = own_rows.shape[0]
    head_count = own_rows.shape[1] // HEAD_DIM
    source_rows = jnp.concatenate([prior_rows, own_rows], axis=0)
    queries = (own_rows.astype(jnp.float32) * query_gain.astype(jnp.float32)).astype(jnp.bfloat16)
    key_rows = (source_rows.astype(jnp.float32) * key_gain.astype(jnp.float32)).astype(jnp.bfloat16)
    queries = queries.reshape(tok_rows, head_count, HEAD_DIM)
    key_rows = key_rows.reshape(2 * tok_rows, head_count, HEAD_DIM)
    value_rows = source_rows.reshape(2 * tok_rows, head_count, HEAD_DIM)
    scores = jnp.einsum(
        "qhd,khd->hqk", queries, key_rows, preferred_element_type=jnp.float32
    ) * HEAD_DIM ** (-0.5)
    key_ids = jnp.concatenate([prior_ids, own_ids], axis=0)
    query_places = jnp.arange(tok_rows, dtype=jnp.int32)
    key_places = jnp.arange(2 * tok_rows, dtype=jnp.int32) - tok_rows
    allowed = (own_ids[:, None] == key_ids[None, :]) & (
        key_places[None, :] <= query_places[:, None]
    )
    scores = jnp.where(allowed[None], scores, -1e30)
    scores = scores - jnp.max(scores, axis=2, keepdims=True)
    raised = jnp.exp(scores)
    weights = (raised / jnp.sum(raised, axis=2, keepdims=True)).astype(jnp.bfloat16)
    mixed = jnp.einsum("hqk,khd->qhd", weights, value_rows, preferred_element_type=jnp.float32)
    return mixed.astype(jnp.bfloat16).reshape(tok_rows, head_count * HEAD_DIM)


def layer(
    current,
    documents,
    chosen,
    attn_gain,
    query_gain,
    key_gain,
    ffn_gain,
    router,
    weight_in,
    weight_out,
):
    tok_rows, model_width = current.shape
    top_count = chosen.shape[1]
    experts = router.shape[1]
    capacity = min(tok_rows, 3 * tok_rows * top_count // (2 * experts))
    normed = rms_norm(current, attn_gain).astype(jnp.bfloat16)
    own_ids = documents + 1
    dp_count = lax.axis_size("dp")
    share_width = model_width // dp_count
    col_start = lax.axis_index("dp") * share_width
    own_rows = lax.dynamic_slice_in_dim(normed, col_start, share_width, 1)
    query_part = lax.dynamic_slice_in_dim(query_gain, col_start, share_width, 0)
    key_part = lax.dynamic_slice_in_dim(key_gain, col_start, share_width, 0)
    prior_rows, prior_ids = shifted((own_rows, own_ids), "expert", 1)
    mixed_part = attend(own_rows, prior_rows, own_ids, prior_ids, query_part, key_part)
    mixed = lax.all_gather(mixed_part, "dp", axis=1, tiled=True)
    residual = current.astype(jnp.float32) + mixed.astype(jnp.float32)
    moe_in = rms_norm(residual, ffn_gain).astype(jnp.bfloat16)
    logits = jnp.dot(moe_in, router, preferred_element_type=jnp.float32)
    chances = jax.nn.softmax(logits, axis=-1)
    picked = jnp.take_along_axis(chances, chosen, axis=1)
    gate_weights = picked / jnp.sum(picked, axis=1, keepdims=True)
    labels = jnp.arange(experts, dtype=jnp.int32)
    member = jnp.sum((chosen[:, :, None] == labels).astype(jnp.int32), axis=1, dtype=jnp.int32)
    ranking = jnp.cumsum(member, axis=0, dtype=jnp.int32) - member
    slot_index = jnp.take_along_axis(ranking, chosen, axis=1)
    positions = chosen * capacity + slot_index
    buffer = jnp.zeros((experts * capacity, model_width), jnp.bfloat16)
    buffer = buffer.at[positions.reshape(-1)].set(jnp.repeat(moe_in, top_count, axis=0))
    grouped = buffer.reshape(experts, capacity, model_width)
    arrived = lax.all_to_all(grouped, "expert", split_axis=0, concat_axis=0, tiled=True)
    rows_in = arrived.reshape(experts * capacity, model_width)
    projected = jnp.dot(
        rows_in, weight_in.reshape(model_width, -1), preferred_element_type=jnp.float32
    )
    half_width = projected.shape[1] // 2
    inner_act = (jax.nn.silu(projected[:, :half_width]) * projected[:, half_width:]).astype(
        jnp.bfloat16
    )
    summed = lax.psum_scatter(
        jnp.dot(inner_act, weight_out, preferred_element_type=jnp.float32),
        "dp",
        scatter_dimension=0,
        tiled=True,
    )
    expert_rows = lax.all_gather(summed.astype(jnp.bfloat16), "dp", axis=0, tiled=True)
    returned = lax.all_to_all(
        expert_rows.reshape(experts, capacity, model_width),
        "expert",
        split_axis=0,
        concat_axis=0,
        tiled=True,
    )
    returned = returned.reshape(experts * capacity, model_width)
    picked_rows = returned[positions]
    combined = jnp.sum(gate_weights[:, :, None] * picked_rows.astype(jnp.float32), axis=1)
    return (residual + combined).astype(jnp.bfloat16)


def body(
    hidden_held,
    fresh_rows,
    doc_held,
    doc_fresh,
    routes,
    attn_gain,
    query_gain,
    key_gain,
    ffn_gain,
    router,
    weight_in,
    weight_out,
):
    tick_count = routes.shape[0]
    phase_first = lax.axis_index("section") == 0
    current = hidden_held[0]
    documents = doc_held[0]
    results = []
    for step_index in range(tick_count):
        made = layer(
            current,
            documents,
            routes[step_index, 0],
            attn_gain[0],
            query_gain[0],
            key_gain[0],
            ffn_gain[0],
            router[0],
            weight_in[0, 0],
            weight_out[0, 0],
        )
        results.append(made)
        if step_index + 1 < tick_count:
            passed, passed_ids = shifted((made, documents), "section", 1)
            current = jnp.where(phase_first, fresh_rows[step_index], passed)
            documents = jnp.where(phase_first, doc_fresh[step_index], passed_ids)
    return jnp.stack(results)[:, None]


def solution(mesh):
    in_specs = (
        P("section", "expert", None),
        P(None, "expert", None),
        P("section", "expert"),
        P(None, "expert"),
        P(None, "section", "expert", None),
        P("section", None),
        P("section", None),
        P("section", None),
        P("section", None),
        P("section", None, None),
        P("section", "expert", None, None, "dp"),
        P("section", "expert", "dp", None),
    )
    out_specs = P(None, "section", "expert", None)
    return jax.shard_map(body, mesh=mesh, in_specs=in_specs, out_specs=out_specs, check_vma=False)
```

profile of v0, /device:TPU:3, one launch (start us, length us, event | category | flops | bytes accessed | tf_op | source)
XLA Modules:
  0.0 775.6 jit_solution(13423039928539818007)
XLA Ops:
  22.6 7.5 collective-permute-done.5
  41.7 25.4 %all-gather.5.cloned.1.call-done = bf16[128,4096]{1,0:T(8,128)(2,1)} async-done(((bf16[128,2048]{1,0:T(8,128)(2,1)}), bf16[128,4096]{1,0:T(8,128)(2,1)}) %all-gather.5.cloned.1.call-update) | async-done | bytes 1048592 | tf_op jit(solution)/shard_map/all_gather | solution.py:76
  74.7 5.5 scatter_custom_fusion
  82.9 8.0 %all-to-all-start = ((bf16[32,12,4096]{2,1,0:T(8,128)(2,1)}), bf16[32,12,4096]{2,1,0:T(8,128)(2,1)}, u32[]{:S(2)}, u32[]{:S(2)}) async-start(bf16[32,12,4096]{2,1,0:T(8,128)(2,1)} %reshape.302), calls=%async_computation | async-start | bytes 8388608 | tf_op jit(solution)/shard_map/all_to_all | solution.py:91
  90.9 13.1 %copy.80 = bf16[512,8,2,768]{3,1,2,0:T(8,128)(2,1)} copy(bf16[512,8,2,768]{3,2,1,0:T(2,128)(2,1)} %bitcast.126) | data formatting | bytes 25165824
  104.0 40.5 %all-to-all-done = bf16[32,12,4096]{2,1,0:T(8,128)(2,1)} async-done(((bf16[32,12,4096]{2,1,0:T(8,128)(2,1)}), bf16[32,12,4096]{2,1,0:T(8,128)(2,1)}, u32[]{:S(2)}, u32[]{:S(2)}) %all-to-all-start) | async-done | bytes 3145760 | tf_op jit(solution)/shard_map/all_to_all | solution.py:91
  144.5 4.0 reshape.303
  148.5 8.1 %fusion.97 = f32[384,1536]{1,0:T(8,128)S(1)} fusion(bf16[384,4096]{1,0:T(8,128)(2,1)S(1)} %reshape.303, bf16[4096,1536]{1,0:T(8,128)(2,1)} %bitcast.127), kind=kOutput, calls=%fused_computation.150 | convolution fusion | flops 4831838208 | bytes 18087936 | tf_op jit(solution)/shard_map/dot_general | solution.py:93
  156.6 7.4 fusion.4
  164.0 84.5 %reduce-scatter.3.cloned.1.call-done = f32[192,4096]{1,0:T(8,128)} async-done(((f32[384,4096]{1,0:T(8,128)}), f32[192,4096]{1,0:T(8,128)}) %reduce-scatter.3.cloned.1.call-update) | async-done | bytes 3145744 | tf_op jit(solution)/shard_map/reduce_scatter | solution.py:100
  251.8 48.6 %all-gather.7.cloned.1.call-done = bf16[384,4096]{1,0:T(8,128)(2,1)} async-done(((bf16[192,4096]{1,0:T(8,128)(2,1)}), bf16[384,4096]{1,0:T(8,128)(2,1)}) %all-gather.7.cloned.1.call-update) | async-done | bytes 3145744 | tf_op jit(solution)/shard_map/all_gather | solution.py:106
  300.3 5.5 reshape.304
  305.8 8.1 %all-to-all-start.1 = ((bf16[32,12,4096]{2,1,0:T(8,128)(2,1)}), bf16[32,12,4096]{2,1,0:T(8,128)(2,1)}, u32[]{:S(2)}, u32[]{:S(2)}) async-start(bf16[32,12,4096]{2,1,0:T(8,128)(2,1)} %reshape.304), calls=%async_computation.2 | async-start | bytes 8388608 | tf_op jit(solution)/shard_map/all_to_all | solution.py:107
  317.1 50.6 %all-to-all-done.1 = bf16[32,12,4096]{2,1,0:T(8,128)(2,1)} async-done(((bf16[32,12,4096]{2,1,0:T(8,128)(2,1)}), bf16[32,12,4096]{2,1,0:T(8,128)(2,1)}, u32[]{:S(2)}, u32[]{:S(2)}) %all-to-all-start.1) | async-done | bytes 3145760 | tf_op jit(solution)/shard_map/all_to_all | solution.py:107
  367.6 4.0 reshape.305
  374.8 5.4 reshape.394
  380.2 8.9 %multiply_reduce_fusion.1 = f32[128,4096]{1,0:T(8,128)S(1)} fusion(f32[128,2,4096]{2,1,0:T(2,128)} %reshape.394, f32[128,2]{1,0:T(8,128)S(1)} %fusion.60), kind=kLoop, calls=%fused_computation.15 | loop fusion | flops 1572864 | bytes 6292480 | tf_op jit(solution)/shard_map/reduce_sum | solution.py:116
  390.9 5.9 collective-permute-done.2
  403.1 10.7 %collective-permute-done.3 = bf16[128,2048]{1,0:T(8,128)(2,1)S(1)} collective-permute-done((bf16[128,2048]{1,0:T(8,128)(2,1)S(1)}, bf16[128,2048]{1,0:T(8,128)(2,1)S(1)}, u32[]{:S(2)}, u32[]{:S(2)}) %collective-permute-start.3) | collective-permute-done | bytes 524320 | tf_op jit(solution)/shard_map/ppermute | solution.py:12
  429.9 23.0 %all-gather.9.cloned.1.call-done = bf16[128,4096]{1,0:T(8,128)(2,1)} async-done(((bf16[128,2048]{1,0:T(8,128)(2,1)}), bf16[128,4096]{1,0:T(8,128)(2,1)}) %all-gather.9.cloned.1.call-update) | async-done | bytes 1048592 | tf_op jit(solution)/shard_map/all_gather | solution.py:76
  460.4 5.5 scatter_custom_fusion.1
  468.6 57.8 %all_to_all.20 = bf16[32,12,4096]{2,1,0:T(8,128)(2,1)} all-to-all(bf16[32,12,4096]{2,1,0:T(8,128)(2,1)} %reshape.311), channel_id=1, replica_groups=mesh['section'=2,'expert'=32,'dp'=2] {'expert'}, dimensions={0} | all-to-all | bytes 6291456 | tf_op jit(solution)/shard_map/all_to_all | solution.py:91
  526.4 4.0 reshape.312
  530.4 8.1 %fusion.98 = f32[384,1536]{1,0:T(8,128)S(1)} fusion(bf16[384,4096]{1,0:T(8,128)(2,1)S(1)} %reshape.312, bf16[4096,1536]{1,0:T(8,128)(2,1)} %bitcast.128), kind=kOutput, calls=%fused_computation.151 | convolution fusion | flops 4831838208 | bytes 18087936 | tf_op jit(solution)/shard_map/dot_general | solution.py:93
  538.5 7.4 fusion.2
  546.0 79.1 %reduce-scatter.5.cloned.1.call-done = f32[192,4096]{1,0:T(8,128)} async-done(((f32[384,4096]{1,0:T(8,128)}), f32[192,4096]{1,0:T(8,128)}) %reduce-scatter.5.cloned.1.call-update) | async-done | bytes 3145744 | tf_op jit(solution)/shard_map/reduce_scatter | solution.py:100
  628.3 48.6 %all-gather.11.cloned.1.call-done = bf16[384,4096]{1,0:T(8,128)(2,1)} async-done(((bf16[192,4096]{1,0:T(8,128)(2,1)}), bf16[384,4096]{1,0:T(8,128)(2,1)}) %all-gather.11.cloned.1.call-update) | async-done | bytes 3145744 | tf_op jit(solution)/shard_map/all_gather | solution.py:106
  676.9 5.5 reshape.313
  682.4 8.1 %all-to-all-start.3 = ((bf16[32,12,4096]{2,1,0:T(8,128)(2,1)}), bf16[32,12,4096]{2,1,0:T(8,128)(2,1)}, u32[]{:S(2)}, u32[]{:S(2)}) async-start(bf16[32,12,4096]{2,1,0:T(8,128)(2,1)} %reshape.313), calls=%async_computation.5 | async-start | bytes 8388608 | tf_op jit(solution)/shard_map/all_to_all | solution.py:107
  693.5 50.6 %all-to-all-done.3 = bf16[32,12,4096]{2,1,0:T(8,128)(2,1)} async-done(((bf16[32,12,4096]{2,1,0:T(8,128)(2,1)}), bf16[32,12,4096]{2,1,0:T(8,128)(2,1)}, u32[]{:S(2)}, u32[]{:S(2)}) %all-to-all-start.3) | async-done | bytes 3145760 | tf_op jit(solution)/shard_map/all_to_all | solution.py:107
  751.3 5.4 reshape.395
  756.7 8.9 %multiply_reduce_fusion = f32[128,4096]{1,0:T(8,128)S(1)} fusion(f32[128,2,4096]{2,1,0:T(2,128)} %reshape.395, f32[128,2]{1,0:T(8,128)S(1)} %fusion.62), kind=kLoop, calls=%fused_computation.14 | loop fusion | flops 1572864 | bytes 6292480 | tf_op jit(solution)/shard_map/reduce_sum | solution.py:116
  (178 shorter events, 97.5 us)
Async XLA Ops:
  6.5 307.6 %copy-start = (bf16[1,4096,32]{1,2,0:T(8,128)(2,1)S(1)}, bf16[1,4096,32]{1,2,0:T(8,128)(2,1)}, u32[]{:S(2)}) copy-start(bf16[1,4096,32]{1,2,0:T(8,128)(2,1)} %param.25) | copy-start | bytes 786436
  6.5 60.5 %all-gather.5.cloned.1.call-start = ((), (), s32[]{:S(2)}) async-start(), calls=%async_computation.6 | async-start | bytes 1572864 | tf_op jit(solution)/shard_map/all_gather | solution.py:76
  7.2 15.3 %collective-permute-start.1 = (s32[128]{0:T(128)S(1)}, s32[128]{0:T(128)S(1)}, u32[]{:S(2)}, u32[]{:S(2)}) collective-permute-start(s32[128]{0:T(128)S(1)} %broadcast_add_fusion), channel_id=1, source_target_pairs={{0,2},{2,4},{4,6},{6,8},{8,10},{10,12},{12,14},{14,16},{16,18},{18... | collective-permute-start | bytes 1544 | tf_op jit(solution)/shard_map/ppermute | solution.py:12
  10.4 8.9 %collective-permute-start.4 = (s32[128]{0:T(128)}, s32[128]{0:T(128)S(1)}, u32[]{:S(2)}, u32[]{:S(2)}) collective-permute-start(s32[128]{0:T(128)} %bitcast.149), channel_id=1, source_target_pairs={{0,64},{1,65},{2,66},{3,67},{4,68},{5,69},{6,70},{7,71},{8,72},{9,... | collective-permute-start | bytes 1544 | tf_op jit(solution)/shard_map/ppermute | solution.py:12
  13.3 5.7 copy-start.27
  14.7 4.6 copy-start.29
  15.9 14.9 %collective-permute-start = (bf16[128,2048]{1,0:T(8,128)(2,1)S(1)}, bf16[128,2048]{1,0:T(8,128)(2,1)S(1)}, u32[]{:S(2)}, u32[]{:S(2)}) collective-permute-start(bf16[128,2048]{1,0:T(8,128)(2,1)S(1)} %get-tuple-element.16), channel_id=1, source_target_pairs={{0,2},{2,4},{4,6},{6,8},{8,10},{10,12},{12,14},{14,16},{16,18},{18... | collective-permute-start | bytes 1572872 | tf_op jit(solution)/shard_map/ppermute | solution.py:12
  19.0 12.6 %copy-start.24 = (f32[1,2048]{1,0:T(1,128)}, f32[1,2048]{1,0:T(1,128)S(1)}, u32[]{:S(2)}) copy-start(f32[1,2048]{1,0:T(1,128)S(1)} %dynamic-slice_convert_fusion) | copy-start | bytes 24580
  19.4 10.7 %collective-permute-start.5 = (s32[128]{0:T(128)S(1)}, s32[128]{0:T(128)S(1)}, u32[]{:S(2)}, u32[]{:S(2)}) collective-permute-start(s32[128]{0:T(128)S(1)} %fusion.68), channel_id=1, source_target_pairs={{0,2},{2,4},{4,6},{6,8},{8,10},{10,12},{12,14},{14,16},{16,18},{18... | collective-permute-start | bytes 1544 | tf_op jit(solution)/shard_map/ppermute | solution.py:12
  38.2 30.7 %copy-start.17 = (f32[1,4096]{1,0:T(1,128)}, f32[1,4096]{1,0:T(1,128)S(1)}, u32[]{:S(2)}) copy-start(f32[1,4096]{1,0:T(1,128)S(1)} %mul.214) | copy-start | bytes 49156
  38.9 28.2 %copy-start.3 = (bf16[1,128,4096]{2,1,0:T(8,128)(2,1)S(1)}, bf16[1,128,4096]{2,1,0:T(8,128)(2,1)}, u32[]{:S(2)}) copy-start(bf16[1,128,4096]{2,1,0:T(8,128)(2,1)} %param.16) | copy-start | bytes 3145732
  82.9 61.7 %all-to-all-start = ((bf16[32,12,4096]{2,1,0:T(8,128)(2,1)}), bf16[32,12,4096]{2,1,0:T(8,128)(2,1)}, u32[]{:S(2)}, u32[]{:S(2)}) async-start(bf16[32,12,4096]{2,1,0:T(8,128)(2,1)} %reshape.302), calls=%async_computation | async-start | bytes 8388608 | tf_op jit(solution)/shard_map/all_to_all | solution.py:91
  90.9 157.7 %reduce-scatter.3.cloned.1.call-start = ((), (), s32[]{:S(2)}) async-start(), calls=%async_computation.7 | async-start | bytes 9437184 | tf_op jit(solution)/shard_map/reduce_scatter | solution.py:100
  164.0 136.4 %all-gather.7.cloned.1.call-start = ((), (), s32[]{:S(2)}) async-start(), calls=%async_computation.8 | async-start | bytes 4718592 | tf_op jit(solution)/shard_map/all_gather | solution.py:106
  305.8 8.3 %copy-start.10 = (bf16[128,4096]{1,0:T(8,128)(2,1)S(1)}, bf16[128,4096]{1,0:T(8,128)(2,1)}, u32[]{:S(2)}) copy-start(bf16[128,4096]{1,0:T(8,128)(2,1)} %copy-done.9) | copy-start | bytes 3145732
  305.8 61.8 %all-to-all-start.1 = ((bf16[32,12,4096]{2,1,0:T(8,128)(2,1)}), bf16[32,12,4096]{2,1,0:T(8,128)(2,1)}, u32[]{:S(2)}, u32[]{:S(2)}) async-start(bf16[32,12,4096]{2,1,0:T(8,128)(2,1)} %reshape.304), calls=%async_computation.2 | async-start | bytes 8388608 | tf_op jit(solution)/shard_map/all_to_all | solution.py:107
  314.0 138.9 %all-gather.9.cloned.1.call-start = ((), (), s32[]{:S(2)}) async-start(), calls=%async_computation.9 | async-start | bytes 1572864 | tf_op jit(solution)/shard_map/all_gather | solution.py:76
  380.2 8.9 %copy-start.4 = (bf16[1,128,4096]{2,1,0:T(8,128)(2,1)S(1)}, bf16[1,128,4096]{2,1,0:T(8,128)(2,1)}, u32[]{:S(2)}) copy-start(bf16[1,128,4096]{2,1,0:T(8,128)(2,1)} %param.16) | copy-start | bytes 3145732
  380.2 8.9 %copy-start.8 = (bf16[128,4096]{1,0:T(8,128)(2,1)S(1)}, bf16[128,4096]{1,0:T(8,128)(2,1)}, u32[]{:S(2)}) copy-start(bf16[128,4096]{1,0:T(8,128)(2,1)} %all-gather.5.cloned.1.call-done) | copy-start | bytes 3145732
  389.1 7.7 copy-start.15
  389.5 7.8 copy-start.13
  389.5 7.8 %copy-start.20 = (f32[2048]{0:T(1024)S(1)}, f32[2048]{0:T(1024)}, u32[]{:S(2)}) copy-start(f32[2048]{0:T(1024)} %copy-done.19) | copy-start | bytes 24580
  389.5 7.3 collective-permute-start.2
  397.3 57.4 %copy-start.1 = (f32[128,4096]{1,0:T(8,128)}, f32[128,4096]{1,0:T(8,128)S(1)}, u32[]{:S(2)}) copy-start(f32[128,4096]{1,0:T(8,128)S(1)} %get-tuple-element.12) | copy-start | bytes 6291460
  398.5 15.3 %collective-permute-start.3 = (bf16[128,2048]{1,0:T(8,128)(2,1)S(1)}, bf16[128,2048]{1,0:T(8,128)(2,1)S(1)}, u32[]{:S(2)}, u32[]{:S(2)}) collective-permute-start(bf16[128,2048]{1,0:T(8,128)(2,1)S(1)} %get-tuple-element.10), channel_id=1, source_target_pairs={{0,2},{2,4},{4,6},{6,8},{8,10},{10,12},{12,14},{14,16},{16,18},{18... | collective-permute-start | bytes 1572872 | tf_op jit(solution)/shard_map/ppermute | solution.py:12
  426.9 198.2 %reduce-scatter.5.cloned.1.call-start = ((), (), s32[]{:S(2)}) async-start(), calls=%async_computation.10 | async-start | bytes 9437184 | tf_op jit(solution)/shard_map/reduce_scatter | solution.py:100
  429.6 25.1 %copy-start.18 = (f32[1,4096]{1,0:T(1,128)S(1)}, f32[1,4096]{1,0:T(1,128)}, u32[]{:S(2)}) copy-start(f32[1,4096]{1,0:T(1,128)} %copy-done.17) | copy-start | bytes 49156
  545.9 131.0 %all-gather.11.cloned.1.call-start = ((), (), s32[]{:S(2)}) async-start(), calls=%async_computation.11 | async-start | bytes 4718592 | tf_op jit(solution)/shard_map/all_gather | solution.py:106
  682.4 8.3 %copy-start.6 = (bf16[128,4096]{1,0:T(8,128)(2,1)S(1)}, bf16[128,4096]{1,0:T(8,128)(2,1)}, u32[]{:S(2)}) copy-start(bf16[128,4096]{1,0:T(8,128)(2,1)} %copy-done.5) | copy-start | bytes 3145732
  682.4 61.8 %all-to-all-start.3 = ((bf16[32,12,4096]{2,1,0:T(8,128)(2,1)}), bf16[32,12,4096]{2,1,0:T(8,128)(2,1)}, u32[]{:S(2)}, u32[]{:S(2)}) async-start(bf16[32,12,4096]{2,1,0:T(8,128)(2,1)} %reshape.313), calls=%async_computation.5 | async-start | bytes 8388608 | tf_op jit(solution)/shard_map/all_to_all | solution.py:107
  756.7 8.9 %copy-start.2 = (f32[128,4096]{1,0:T(8,128)S(1)}, f32[128,4096]{1,0:T(8,128)}, u32[]{:S(2)}) copy-start(f32[128,4096]{1,0:T(8,128)} %copy-done.1) | copy-start | bytes 6291460
  756.7 8.9 %copy-start.12 = (bf16[128,4096]{1,0:T(8,128)(2,1)S(1)}, bf16[128,4096]{1,0:T(8,128)(2,1)}, u32[]{:S(2)}) copy-start(bf16[128,4096]{1,0:T(8,128)(2,1)} %all-gather.9.cloned.1.call-done) | copy-start | bytes 3145732
  (13 other events, 33.9 us)
Sparse Core Ops, SparseCore 0:
  38.3 28.7 all-gather.4
  164.1 84.3 reduce-scatter.2
  251.9 48.3 all-gather.6
  427.0 25.8 all-gather.8
  546.0 78.9 reduce-scatter.4
  628.4 48.3 all-gather.10
where the time goes:
time: 791 us; the launch traced here: 776 us
  waiting for transfers between devices  475 us (60%)
  local copies, waits for them, and re-layouts  103 us (13%)
  blocking collectives  57.8 us (7%)
  matrix products  43.9 us (6%)
  other arithmetic  40.7 us (5%)
  starting transfers between devices  40.2 us (5%)
  between operations  14.8 us (2%)
    reduce_scatter x2, waiting for transfers between devices, layer(): lax.psum_scatter(jnp.dot(inner_act, weight_out, preferred_element_type=jn...  164 us
    all_to_all x2, waiting for transfers between devices, layer(): lax.all_to_all(expert_rows.reshape(experts, capacity, model_width), 'expe...  101 us
    all_gather x2, waiting for transfers between devices, layer(): lax.all_gather(summed.astype(jnp.bfloat16), 'dp', axis=0, tiled=True)  97.1 us
    all_to_all x1, blocking collectives, layer(): lax.all_to_all(grouped, 'expert', split_axis=0, concat_axis=0, tiled=True)  57.8 us
    all_gather x2, waiting for transfers between devices, layer(): mixed = lax.all_gather(mixed_part, 'dp', axis=1, tiled=True)  48.4 us
    all_to_all x1, waiting for transfers between devices, layer(): lax.all_to_all(grouped, 'expert', split_axis=0, concat_axis=0, tiled=True)  40.5 us
    ppermute x6, waiting for transfers between devices, shifted(): return lax.ppermute(array, axis, pairs)  24 us
    reduce_sum x2, other arithmetic, layer(): jnp.sum(gate_weights[:, :, None] * picked_rows.astype(jnp.float32), axis=1)  17.8 us
  transfers between devices with their start and end apart: 15, of which 12 were waited for; matrix products, arithmetic and copies ran while one was open for 4% of the time, Pallas kernels for 0%

commit v1 on v0

v1 whole, which is shorter than its diff:
```python
import jax
import jax.numpy as jnp
import numpy as np
from jax import lax
from jax.experimental import pallas as pl
from jax.experimental.pallas import tpu as pltpu
from jax.sharding import PartitionSpec as P

MESH = pl.DeviceIdType.MESH
BF = jnp.bfloat16
F32 = jnp.float32
TOK = 128
D = 4096
HALF = 2048
CH = 512
NCH = HALF // CH
EXP = 32
CAP = 12
MSG = CAP * NCH
ROWS = EXP * MSG
QUAD = 4 * MSG
SLOTS = EXP * CAP
HID = 768
EPS = 1e-06


def _constants():
    row = np.arange(ROWS)
    chunk = (row % MSG) // CAP
    key = (row // MSG) * CAP + row % CAP + 1024 * chunk
    key_col = np.broadcast_to(key[:, None], (ROWS, TOK)).astype(np.float32)
    key_row = np.broadcast_to(key[None, :], (8, ROWS)).astype(np.float32)
    sort = np.zeros((QUAD, QUAD), np.float32)
    for j in range(4):
        for c in range(NCH):
            for slot in range(CAP):
                sort[c * 48 + j * CAP + slot, j * MSG + c * CAP + slot] = 1.0
    before = np.triu(np.ones((TOK, TOK), np.float32), 1)
    return key_col, key_row, sort, sort.T.copy(), before


def _kernel(
    held,
    fresh,
    ids_held,
    ids_fresh,
    routes,
    attn_gain,
    query_gain,
    key_gain,
    ffn_gain,
    router,
    w_in_hbm,
    w_out_hbm,
    key_col,
    key_row,
    sort,
    unsort,
    before,
    out_hbm,
    w_in,
    w_out,
    recv_d,
    recv_c,
    send_d,
    send_c,
    rows_in,
    inner,
    staged,
    pick,
    comb,
    cur,
    normed,
    prior,
    res,
    moe,
    carry,
    out_half,
    sums,
    stat_send,
    stat_recv,
    row_send,
    row_recv,
    ids_own,
    ids_pri,
    s_w,
    s_ids_send,
    s_ids_recv,
    s_prior_send,
    s_prior_recv,
    s_stat_send,
    s_stat_recv,
    s_carry,
    s_row_send,
    s_row_recv,
    s_d_send,
    s_d_recv,
    s_c_send,
    s_c_recv,
    s_out,
    s_out_recv,
):
    s = lax.axis_index("section")
    e = lax.axis_index("expert")
    h = lax.axis_index("dp")
    z, y, xl = e // 8, (e // 2) % 4, e % 2
    x = h * 2 + xl
    start_col = pl.multiple_of(h * HALF, HALF)

    def at(section, expert, dp):
        return {"section": section, "expert": expert, "dp": dp}

    def offset(j):
        k = (13 * j) % 32
        return k % 2, (k // 2) % 4, k // 8

    def ahead(m):
        dx, dy, dz = offset(m // 2)
        x2 = (x + dx + 2 * (m % 2)) % 4
        return ((z + dz) % 4) * 8 + ((y + dy) % 4) * 2 + x2 % 2, x2 // 2

    def behind(j):
        dx, dy, dz = offset(j)
        return ((z + 4 - dz) % 4) * 8 + ((y + 4 - dy) % 4) * 2 + (xl + dx) % 2

    nxt, prv = (e + 1) % EXP, (e + EXP - 1) % EXP

    load_in = pltpu.make_async_copy(w_in_hbm, w_in, s_w.at[0])
    load_out = pltpu.make_async_copy(w_out_hbm, w_out, s_w.at[1])
    load_in.start()
    load_out.start()

    barrier = pltpu.get_barrier_semaphore()

    @pl.loop(1, 2 * EXP)
    def _(m):
        e2, h2 = ahead(m)
        pl.semaphore_signal(barrier, inc=1, device_id=at(s, e2, h2), device_id_type=MESH)

    for e2, h2 in ((e, h), (e, 1 - h), (nxt, h), (prv, h)):
        pl.semaphore_signal(barrier, inc=1, device_id=at(1 - s, e2, h2), device_id_type=MESH)

    ids_own[0] = jnp.broadcast_to(ids_held[...], (8, TOK))

    @pl.when(s == 0)
    def _():
        ids_own[1] = jnp.broadcast_to(ids_fresh[...], (8, TOK))

    pl.semaphore_wait(barrier, 2 * EXP - 1 + 4)

    def send_ids(src, dst, i, j, device):
        return pltpu.make_async_remote_copy(
            src_ref=src,
            dst_ref=dst,
            send_sem=s_ids_send.at[i],
            recv_sem=s_ids_recv.at[j],
            device_id=device,
            device_id_type=MESH,
        )

    ids_0 = send_ids(ids_own.at[0], ids_pri.at[0], 0, 0, at(s, nxt, h))
    ids_1 = send_ids(ids_own.at[1], ids_pri.at[1], 1, 1, at(0, nxt, h))
    ids_2 = send_ids(ids_own.at[0], ids_own.at[1], 2, 2, at(1, e, h))
    ids_3 = send_ids(ids_own.at[0], ids_pri.at[1], 3, 1, at(1, nxt, h))
    ids_0.start()

    @pl.when(s == 0)
    def _():
        ids_1.start()
        ids_2.start()
        ids_3.start()

    def head_cols(c):
        return pl.ds(pl.multiple_of(c * TOK, TOK), TOK)

    def own_cols(c):
        return pl.ds(pl.multiple_of(start_col + c * TOK, TOK), TOK)

    def take_input(ref):
        sums[...] = jnp.zeros((TOK, TOK), F32)

        @pl.loop(0, D // TOK, unroll=8)
        def _(c):
            wide = ref[:, head_cols(c)].astype(F32)
            sums[...] += wide * wide

        cur[...] = ref[:, pl.ds(start_col, HALF)]

    @pl.loop(0, 2)
    def _(t):
        @pl.when(t == 0)
        def _():
            take_input(held)

        @pl.when((t == 1) & (s == 0))
        def _():
            take_input(fresh)

        @pl.when((t == 1) & (s == 1))
        def _():
            pltpu.make_async_remote_copy(
                src_ref=out_half.at[0],
                dst_ref=carry,
                send_sem=s_carry.at[0],
                recv_sem=s_carry.at[1],
                device_id=at(1, e, h),
                device_id_type=MESH,
            ).wait_recv()
            for i in range(2):
                pltpu.make_async_remote_copy(
                    src_ref=row_send,
                    dst_ref=row_recv.at[i],
                    send_sem=s_row_send.at[i],
                    recv_sem=s_row_recv.at[i],
                    device_id=at(1, e, h),
                    device_id_type=MESH,
                ).wait_recv()
            sums[...] = row_recv[0] + row_recv[1]
            cur[...] = carry[...]

        scale = lax.rsqrt(jnp.sum(sums[...], axis=1, keepdims=True) * (1.0 / D) + EPS)

        @pl.loop(0, HALF // TOK, unroll=4)
        def _(c):
            wide = cur[:, head_cols(c)].astype(F32)
            gain = attn_gain[:, own_cols(c)].astype(F32)
            normed[t, :, head_cols(c)] = (wide * scale * gain).astype(BF)

        send_prior = pltpu.make_async_remote_copy(
            src_ref=normed.at[t],
            dst_ref=prior.at[t],
            send_sem=s_prior_send.at[t],
            recv_sem=s_prior_recv.at[t],
            device_id=at(s, nxt, h),
            device_id_type=MESH,
        )
        send_prior.start()

        chosen = routes[t]
        label = lax.broadcasted_iota(jnp.int32, (EXP, TOK), 0)
        first = (label == chosen[0:1]).astype(F32)
        second = (label == chosen[1:2]).astype(F32)
        ranking = jnp.dot((first + second).astype(BF), before[...], preferred_element_type=F32)
        place_0 = jnp.sum((ranking + label.astype(F32) * CAP) * first, axis=0, keepdims=True)
        place_1 = jnp.sum((ranking + label.astype(F32) * CAP) * second, axis=0, keepdims=True)

        @pl.loop(0, ROWS // TOK)
        def _(r):
            rows = pl.ds(pl.multiple_of(r * TOK, TOK), TOK)
            keys = key_col[rows, :]
            for c in range(NCH):
                hit = (keys == place_0 + 1024.0 * c) | (keys == place_1 + 1024.0 * c)
                pick[rows, c * TOK : (c + 1) * TOK] = hit.astype(F32).astype(BF)

        @pl.when((t == 1) & (s == 1))
        def _():
            ids_2.wait_recv()

        @pl.when(t == 0)
        def _():
            ids_0.wait_recv()

        @pl.when(t == 1)
        def _():
            ids_1.wait_recv()

        row_ids = jnp.broadcast_to(ids_own[t, 0:1, :].astype(F32), (TOK, TOK))
        prior_ids = jnp.broadcast_to(ids_pri[t, 0:1, :].astype(F32), (TOK, TOK))
        col_ids = jnp.transpose(row_ids)
        causal = lax.broadcasted_iota(jnp.int32, (TOK, TOK), 1) <= lax.broadcasted_iota(
            jnp.int32, (TOK, TOK), 0
        )
        own_mask = jnp.where((col_ids == row_ids) & causal, 0.0, -1e30)
        pri_mask = jnp.where((col_ids == prior_ids) & (e > 0), 0.0, -1e30)
        send_prior.wait_recv()
        sums[...] = jnp.zeros((TOK, TOK), F32)

        @pl.loop(0, HALF // TOK // 4)
        def _(quad):
            for i in range(4):
                c = quad * 4 + i
                own = normed[t, :, head_cols(c)]
                pri = prior[t, :, head_cols(c)]
                q_gain = query_gain[:, own_cols(c)].astype(F32)
                k_gain = key_gain[:, own_cols(c)].astype(F32)
                queries = (own.astype(F32) * q_gain).astype(BF)
                own_keys = (own.astype(F32) * k_gain).astype(BF)
                pri_keys = (pri.astype(F32) * k_gain).astype(BF)
                dims = (((1,), (1,)), ((), ()))
                own_s = lax.dot_general(queries, own_keys, dims, preferred_element_type=F32)
                pri_s = lax.dot_general(queries, pri_keys, dims, preferred_element_type=F32)
                own_s = own_s * TOK**-0.5 + own_mask
                pri_s = pri_s * TOK**-0.5 + pri_mask
                top = jnp.max(jnp.maximum(own_s, pri_s), axis=1, keepdims=True)
                own_p = jnp.exp(own_s - top)
                pri_p = jnp.exp(pri_s - top)
                total = jnp.sum(own_p + pri_p, axis=1, keepdims=True)
                share = 1.0 / total
                mixed = jnp.dot((own_p * share).astype(BF), own, preferred_element_type=F32)
                mixed += jnp.dot((pri_p * share).astype(BF), pri, preferred_element_type=F32)
                summed = cur[:, head_cols(c)].astype(F32) + mixed.astype(BF).astype(F32)
                res[:, head_cols(c)] = summed
                sums[...] += summed * summed
                f_gain = ffn_gain[:, own_cols(c)].astype(F32)
                moe[:, head_cols(c)] = (summed * f_gain).astype(BF)

        stat_send[t, 0:TOK, :] = sums[...]
        stat_send[t, TOK:, :] = lax.dot_general(
            router[:, pl.ds(start_col, HALF)],
            moe[...],
            (((1,), (1,)), ((), ())),
            preferred_element_type=F32,
        )
        send_stat = pltpu.make_async_remote_copy(
            src_ref=stat_send.at[t],
            dst_ref=stat_recv.at[t],
            send_sem=s_stat_send.at[t],
            recv_sem=s_stat_recv.at[t],
            device_id=at(s, e, 1 - h),
            device_id_type=MESH,
        )
        send_stat.start()
        send_stat.wait_recv()
        sums[...] = stat_send[t, 0:TOK, :] + stat_recv[t, 0:TOK, :]
        logits = stat_send[t, TOK:, :] + stat_recv[t, TOK:, :]
        scale = lax.rsqrt(jnp.sum(sums[...], axis=1, keepdims=True) * (1.0 / D) + EPS)

        @pl.loop(0, HALF // TOK, unroll=4)
        def _(c):
            f_gain = ffn_gain[:, own_cols(c)].astype(F32)
            moe[:, head_cols(c)] = (res[:, head_cols(c)] * scale * f_gain).astype(BF)

        @pl.when(t == 1)
        def _():
            @pl.loop(1, 2 * EXP)
            def _(m):
                pltpu.make_async_remote_copy(
                    src_ref=send_d.at[pl.ds(0, MSG)],
                    dst_ref=recv_d.at[0, 0, 0, pl.ds(0, MSG)],
                    send_sem=s_d_send.at[m],
                    recv_sem=s_d_recv.at[0, 0],
                    device_id=at(s, nxt, h),
                    device_id_type=MESH,
                ).wait_send()

        @pl.loop(0, EXP // 4)
        def _(g):
            rows = pl.ds(pl.multiple_of(g * QUAD, QUAD), QUAD)
            total = jnp.zeros((QUAD, CH), F32)
            for c in range(NCH):
                total += jnp.dot(
                    pick[rows, c * TOK : (c + 1) * TOK],
                    moe[:, c * CH : (c + 1) * CH],
                    preferred_element_type=F32,
                )
            send_d[rows, :] = total.astype(BF)

        @pl.loop(1, 2 * EXP)
        def _(m):
            e2, h2 = ahead(m)
            j = m // 2
            pltpu.make_async_remote_copy(
                src_ref=send_d.at[pl.ds(pl.multiple_of(e2 * MSG, MSG), MSG)],
                dst_ref=recv_d.at[t, j // 4, h, pl.ds(pl.multiple_of((j % 4) * MSG, MSG), MSG)],
                send_sem=s_d_send.at[m],
                recv_sem=s_d_recv.at[t, j // 4],
                device_id=at(s, e2, h2),
                device_id_type=MESH,
            ).start()

        pltpu.make_async_copy(
            send_d.at[pl.ds(pl.multiple_of(e * MSG, MSG), MSG)],
            recv_d.at[t, 0, h, pl.ds(0, MSG)],
            s_d_recv.at[t, 0],
        ).start()

        scale_row = jnp.transpose(jnp.broadcast_to(scale, (TOK, TOK)))
        logits = logits * scale_row[0:EXP, :]
        logit_0 = jnp.sum(logits * first, axis=0, keepdims=True)
        logit_1 = jnp.sum(logits * second, axis=0, keepdims=True)
        top = jnp.maximum(logit_0, logit_1)
        raised_0, raised_1 = jnp.exp(logit_0 - top), jnp.exp(logit_1 - top)
        gate_0 = raised_0 / (raised_0 + raised_1)
        gate_1 = raised_1 / (raised_0 + raised_1)

        def column(row):
            return jnp.transpose(jnp.broadcast_to(row, (TOK, TOK)))

        gate_0, gate_1 = column(gate_0), column(gate_1)
        place_0, place_1 = column(place_0), column(place_1)

        @pl.loop(0, ROWS // TOK)
        def _(r):
            cols = pl.ds(pl.multiple_of(r * TOK, TOK), TOK)
            keys = key_row[0:1, cols]
            for c in range(NCH):
                value = jnp.where(keys == place_0 + 1024.0 * c, gate_0, 0.0)
                value += jnp.where(keys == place_1 + 1024.0 * c, gate_1, 0.0)
                comb[c, :, cols] = value.astype(BF)

        @pl.when(t == 0)
        def _():
            load_in.wait()
            load_out.wait()

        @pl.loop(0, EXP // 4)
        def _(g):
            pltpu.make_async_copy(
                recv_d.at[t, g], recv_d.at[t, g], s_d_recv.at[t, g]
            ).wait()
            for p in range(2):
                sorted_rows = jnp.dot(
                    sort[...], recv_d[t, g, p], preferred_element_type=F32
                ).astype(BF)
                for c in range(NCH):
                    rows_in[
                        pl.ds(pl.multiple_of(g * 48, 48), 48),
                        p * HALF + c * CH : p * HALF + (c + 1) * CH,
                    ] = sorted_rows[c * 48 : (c + 1) * 48]

        @pl.loop(0, HID // 256)
        def _(n):
            gate = jnp.dot(
                rows_in[...],
                w_in[:, pl.ds(pl.multiple_of(n * 256, 256), 256)],
                preferred_element_type=F32,
            )
            up = jnp.dot(
                rows_in[...],
                w_in[:, pl.ds(pl.multiple_of(HID + n * 256, 256), 256)],
                preferred_element_type=F32,
            )
            inner[:, pl.ds(pl.multiple_of(n * 256, 256), 256)] = (
                gate / (1.0 + jnp.exp(-gate)) * up
            ).astype(BF)

        @pl.when(t == 1)
        def _():
            @pl.loop(1, 2 * EXP)
            def _(m):
                pltpu.make_async_remote_copy(
                    src_ref=send_c.at[0, pl.ds(0, MSG)],
                    dst_ref=recv_c.at[0, 0, pl.ds(0, MSG)],
                    send_sem=s_c_send.at[m],
                    recv_sem=s_c_recv.at[0],
                    device_id=at(s, nxt, h),
                    device_id_type=MESH,
                ).wait_send()

        @pl.loop(0, 2)
        def _(p):
            for c in range(NCH):
                col = pl.multiple_of(p * HALF + c * CH, CH)
                staged[c] = jnp.dot(
                    inner[...], w_out[:, pl.ds(col, CH)], preferred_element_type=F32
                ).astype(BF)

            @pl.loop(0, EXP // 4)
            def _(g):
                rows = pl.ds(pl.multiple_of(g * 48, 48), 48)
                stack = staged[:, rows, :].reshape(QUAD, CH)
                packed = jnp.dot(unsort[...], stack, preferred_element_type=F32)
                send_c[p, pl.ds(pl.multiple_of(g * QUAD, QUAD), QUAD), :] = packed.astype(BF)

                @pl.loop(0, 4)
                def _(i):
                    j = g * 4 + i
                    remote = (j > 0) | (p != h)
                    src = send_c.at[p, pl.ds(pl.multiple_of(j * MSG, MSG), MSG)]
                    dst = recv_c.at[t, h, pl.ds(pl.multiple_of(e * MSG, MSG), MSG)]

                    @pl.when(remote)
                    def _():
                        m = jnp.where(j > 0, j * 2 + p, 1)
                        pltpu.make_async_remote_copy(
                            src_ref=src,
                            dst_ref=dst,
                            send_sem=s_c_send.at[m],
                            recv_sem=s_c_recv.at[t],
                            device_id=at(s, behind(j), p),
                            device_id_type=MESH,
                        ).start()

                    @pl.when(jnp.logical_not(remote))
                    def _():
                        pltpu.make_async_copy(src, dst, s_c_recv.at[t]).start()

        pltpu.make_async_copy(recv_c.at[t], recv_c.at[t], s_c_recv.at[t]).wait()
        sums[...] = jnp.zeros((TOK, TOK), F32)
        for c in range(NCH):
            combined = jnp.dot(comb[c], recv_c[t, 0], preferred_element_type=F32)
            combined += jnp.dot(comb[c], recv_c[t, 1], preferred_element_type=F32)
            final = (res[:, c * CH : (c + 1) * CH] + combined).astype(BF)
            out_half[t, :, c * CH : (c + 1) * CH] = final
            for i in range(CH // TOK):
                wide = final[:, i * TOK : (i + 1) * TOK].astype(F32)
                sums[...] += wide * wide

        @pl.when((t == 0) & (s == 0))
        def _():
            pltpu.make_async_remote_copy(
                src_ref=out_half.at[0],
                dst_ref=carry,
                send_sem=s_carry.at[0],
                recv_sem=s_carry.at[1],
                device_id=at(1, e, h),
                device_id_type=MESH,
            ).start()
            row_send[...] = sums[...]
            for i in range(2):
                pltpu.make_async_remote_copy(
                    src_ref=row_send,
                    dst_ref=row_recv.at[h],
                    send_sem=s_row_send.at[i],
                    recv_sem=s_row_recv.at[h],
                    device_id=at(1, e, (h + i) % 2),
                    device_id_type=MESH,
                ).start()

        half_out = out_hbm.at[t, :, pl.ds(start_col, HALF)]
        pltpu.make_async_copy(out_half.at[t], half_out, s_out.at[t, 0]).start()
        pltpu.make_async_remote_copy(
            src_ref=out_half.at[t],
            dst_ref=half_out,
            send_sem=s_out.at[t, 1],
            recv_sem=s_out_recv.at[t],
            device_id=at(s, e, 1 - h),
            device_id_type=MESH,
        ).start()

    @pl.loop(0, 2)
    def _(t):
        other_out = out_hbm.at[t, :, pl.ds(pl.multiple_of((1 - h) * HALF, HALF), HALF)]
        pltpu.make_async_copy(
            out_half.at[t], out_hbm.at[t, :, pl.ds(start_col, HALF)], s_out.at[t, 0]
        ).wait()
        done = pltpu.make_async_remote_copy(
            src_ref=out_half.at[t],
            dst_ref=other_out,
            send_sem=s_out.at[t, 1],
            recv_sem=s_out_recv.at[t],
            device_id=at(s, e, 1 - h),
            device_id_type=MESH,
        )
        done.wait_send()
        done.wait_recv()
        pltpu.make_async_remote_copy(
            src_ref=normed.at[t],
            dst_ref=prior.at[t],
            send_sem=s_prior_send.at[t],
            recv_sem=s_prior_recv.at[t],
            device_id=at(s, nxt, h),
            device_id_type=MESH,
        ).wait_send()
        pltpu.make_async_remote_copy(
            src_ref=stat_send.at[t],
            dst_ref=stat_recv.at[t],
            send_sem=s_stat_send.at[t],
            recv_sem=s_stat_recv.at[t],
            device_id=at(s, e, 1 - h),
            device_id_type=MESH,
        ).wait_send()

    @pl.loop(1, 2 * EXP)
    def _(m):
        pltpu.make_async_remote_copy(
            src_ref=send_d.at[pl.ds(0, MSG)],
            dst_ref=recv_d.at[0, 0, 0, pl.ds(0, MSG)],
            send_sem=s_d_send.at[m],
            recv_sem=s_d_recv.at[0, 0],
            device_id=at(s, nxt, h),
            device_id_type=MESH,
        ).wait_send()
        pltpu.make_async_remote_copy(
            src_ref=send_c.at[0, pl.ds(0, MSG)],
            dst_ref=recv_c.at[0, 0, pl.ds(0, MSG)],
            send_sem=s_c_send.at[m],
            recv_sem=s_c_recv.at[0],
            device_id=at(s, nxt, h),
            device_id_type=MESH,
        ).wait_send()

    ids_0.wait_send()

    @pl.when(s == 0)
    def _():
        ids_1.wait_send()
        ids_2.wait_send()
        ids_3.wait_send()
        pltpu.make_async_remote_copy(
            src_ref=out_half.at[0],
            dst_ref=carry,
            send_sem=s_carry.at[0],
            recv_sem=s_carry.at[1],
            device_id=at(1, e, h),
            device_id_type=MESH,
        ).wait_send()
        for i in range(2):
            pltpu.make_async_remote_copy(
                src_ref=row_send,
                dst_ref=row_recv.at[h],
                send_sem=s_row_send.at[i],
                recv_sem=s_row_recv.at[h],
                device_id=at(1, e, (h + i) % 2),
                device_id_type=MESH,
            ).wait_send()


def body(
    hidden_held,
    fresh_rows,
    doc_held,
    doc_fresh,
    routes,
    attn_gain,
    query_gain,
    key_gain,
    ffn_gain,
    router,
    weight_in,
    weight_out,
):
    key_col, key_row, sort, unsort, before = _constants()
    vmem = pl.BlockSpec(memory_space=pltpu.VMEM)
    hbm = pl.BlockSpec(memory_space=pl.ANY)
    dma = pltpu.SemaphoreType.DMA
    out = pl.pallas_call(
        _kernel,
        out_shape=jax.ShapeDtypeStruct((2, TOK, D), BF),
        in_specs=[vmem] * 10 + [hbm] * 2 + [vmem] * 5,
        out_specs=hbm,
        scratch_shapes=[
            pltpu.VMEM((D, 2 * HID), BF),
            pltpu.VMEM((HID, D), BF),
            pltpu.VMEM((2, EXP // 4, 2, QUAD, CH), BF),
            pltpu.VMEM((2, 2, ROWS, CH), BF),
            pltpu.VMEM((ROWS, CH), BF),
            pltpu.VMEM((2, ROWS, CH), BF),
            pltpu.VMEM((SLOTS, D), BF),
            pltpu.VMEM((SLOTS, HID), BF),
            pltpu.VMEM((NCH, SLOTS, CH), BF),
            pltpu.VMEM((ROWS, NCH * TOK), BF),
            pltpu.VMEM((NCH, TOK, ROWS), BF),
            pltpu.VMEM((TOK, HALF), BF),
            pltpu.VMEM((2, TOK, HALF), BF),
            pltpu.VMEM((2, TOK, HALF), BF),
            pltpu.VMEM((TOK, HALF), F32),
            pltpu.VMEM((TOK, HALF), BF),
            pltpu.VMEM((TOK, HALF), BF),
            pltpu.VMEM((2, TOK, HALF), BF),
            pltpu.VMEM((TOK, TOK), F32),
            pltpu.VMEM((2, TOK + EXP, TOK), F32),
            pltpu.VMEM((2, TOK + EXP, TOK), F32),
            pltpu.VMEM((TOK, TOK), F32),
            pltpu.VMEM((2, TOK, TOK), F32),
            pltpu.VMEM((2, 8, TOK), jnp.int32),
            pltpu.VMEM((2, 8, TOK), jnp.int32),
            dma((2,)),
            dma((4,)),
            dma((3,)),
            dma((2,)),
            dma((2,)),
            dma((2,)),
            dma((2,)),
            dma((2,)),
            dma((2,)),
            dma((2,)),
            dma((2 * EXP,)),
            dma((2, EXP // 4)),
            dma((2 * EXP,)),
            dma((2,)),
            dma((2, 2)),
            dma((2,)),
        ],
        compiler_params=pltpu.CompilerParams(
            collective_id=0, has_side_effects=True, vmem_limit_bytes=60 << 20
        ),
        cost_estimate=pl.CostEstimate(
            flops=25_000_000_000, bytes_accessed=25_000_000, transcendentals=5_000_000
        ),
    )(
        hidden_held[0],
        fresh_rows[0],
        doc_held,
        doc_fresh,
        jnp.swapaxes(routes[:, 0], 1, 2),
        attn_gain,
        query_gain,
        key_gain,
        ffn_gain,
        router[0].T,
        weight_in.reshape(D, 2 * HID),
        weight_out[0, 0],
        jnp.asarray(key_col),
        jnp.asarray(key_row),
        jnp.asarray(sort, BF),
        jnp.asarray(unsort, BF),
        jnp.asarray(before, BF),
    )
    return out[:, None]


def solution(mesh):
    in_specs = (
        P("section", "expert", None),
        P(None, "expert", None),
        P("section", "expert"),
        P(None, "expert"),
        P(None, "section", "expert", None),
        P("section", None),
        P("section", None),
        P("section", None),
        P("section", None),
        P("section", None, None),
        P("section", "expert", None, None, "dp"),
        P("section", "expert", "dp", None),
    )
    out_specs = P(None, "section", "expert", None)
    return jax.shard_map(body, mesh=mesh, in_specs=in_specs, out_specs=out_specs, check_vma=False)
```

time: 791 us -> 299 us (0.38); the launches traced: 776 us -> 297 us
  waiting for transfers between devices: 475 us -> 0 us
  Pallas kernels: 0 us -> 280 us
  local copies, waits for them, and re-layouts: 103 us -> 16.2 us
  blocking collectives: 57.8 us -> 0 us
  matrix products: 43.9 us -> 0 us
  other arithmetic: 40.7 us -> 0 us
  starting transfers between devices: 40.2 us -> 0 us
  between operations: 14.8 us -> 0.01 us
    pallas_call x0 -> x1, Pallas kernels: none -> 280 us  [body(): pl.pallas_call(_kernel, out_shape=jax.ShapeDtypeStruct((2, TOK, D), BF),...]
    reduce_scatter x2 -> x0, waiting for transfers between devices: 164 us -> none  [layer(): lax.psum_scatter(jnp.dot(inner_act, weight_out, preferred_element_type=jn...]
    all_gather x4 -> x0, waiting for transfers between devices: 145 us -> none  [the longest x2 97.1 us: layer(): lax.all_gather(summed.astype(jnp.bfloat16), 'dp', axis=0, tiled=True)]
    all_to_all x3 -> x0, waiting for transfers between devices: 142 us -> none  [the longest x2 101 us: layer(): lax.all_to_all(expert_rows.reshape(experts, capacity, model_width), 'expe...]
    all_to_all x1 -> x0, blocking collectives: 57.8 us -> none  [layer(): lax.all_to_all(grouped, 'expert', split_axis=0, concat_axis=0, tiled=True)]
    reshape x14 -> x0, local copies, waits for them, and re-layouts: 40 us -> none  [the longest x2 11 us: layer(): expert_rows.reshape(experts, capacity, model_width)]
    dot_general x8 -> x0, matrix products: 37 us -> none  [the longest x2 16.2 us: layer(): jnp.dot(rows_in, weight_in.reshape(model_width, -1), preferred_element_ty...]
    all_to_all x3 -> x0, starting transfers between devices: 24.2 us -> none  [the longest x2 16.2 us: layer(): lax.all_to_all(expert_rows.reshape(experts, capacity, model_width), 'expe...]
  transfers between devices with their start and end apart: 15 -> 0, of which waited for: 12 -> 0; matrix products, arithmetic and copies ran while one was open for 4% -> 0% of each run, Pallas kernels for 0% -> 0%
where the time goes in v1:
time: 299 us; the launch traced here: 297 us
  Pallas kernels  280 us (94%)
  local copies, waits for them, and re-layouts  16.2 us (5%)
    pallas_call x1, Pallas kernels, body(): pl.pallas_call(_kernel, out_shape=jax.ShapeDtypeStruct((2, TOK, D), BF),...  280 us
    unnamed x2, local copies, waits for them, and re-layouts  16.2 us

profile of v1, /device:TPU:3, one launch (start us, length us, event | category | flops | bytes accessed | tf_op | source)
XLA Modules:
  0.0 296.6 jit_solution(221210665620351938)
XLA Ops:
  0.0 13.1 %copy.19 = bf16[512,8,2,768]{3,1,2,0:T(8,128)(2,1)} copy(bf16[512,8,2,768]{3,2,1,0:T(2,128)(2,1)} %bitcast.15) | data formatting | bytes 25165824
  13.1 280.4 %shard_map.163 = bf16[2,128,4096]{2,1,0:T(8,128)(2,1)} custom-call(bf16[128,4096]{1,0:T(8,128)(2,1)} %bitcast.19, bf16[128,4096]{1,0:T(8,128)(2,1)} %bitcast.20, s32[1,128]{1,0:T(1,128)} %ids_held.1, s32[1,128]{1,0:T(1,128)} %ids_fresh.1, s32[2,2,128]{2,1,0:T(2,128)} %bitcast.22, bf16[1,4096]{1,0:T(2,128)(2,1)} %attn_gain.1, bf16[1,4096]{1,0:T(2,128)(2,1)} %query_gain.1, ...), custom_call_target="tpu_custom_call" | custom-call | flops 24999999488 | bytes 25000000 | tf_op jit(solution)/shard_map/pallas_call | solution.py:627
  293.5 3.1 %copy.21 = bf16[2,1,128,4096]{3,2,1,0:T(8,128)(2,1)} copy(bf16[2,1,128,4096]{3,2,1,0:T(8,128)(2,1)} %bitcast.17) | data formatting | bytes 4194304

commit v2 on v1

v2 whole, which is shorter than its diff:
```python
import jax
import jax.numpy as jnp
import numpy as np
from jax import lax
from jax.experimental import pallas as pl
from jax.experimental.pallas import tpu as pltpu
from jax.sharding import PartitionSpec as P

MESH = pl.DeviceIdType.MESH
BF = jnp.bfloat16
F32 = jnp.float32
TOK = 128
D = 4096
HALF = 2048
CH = 512
NCH = HALF // CH
EXP = 32
CAP = 12
MSG = CAP * NCH
ROWS = EXP * MSG
QUAD = 4 * MSG
SLOTS = EXP * CAP
HID = 768
WROWS = 256
EPS = 1e-06


def _constants():
    row = np.arange(ROWS)
    chunk = (row % MSG) // CAP
    key = (row // MSG) * CAP + row % CAP + 1024 * chunk
    key_col = np.broadcast_to(key[:, None], (ROWS, TOK)).astype(np.float32)
    key_row = np.broadcast_to(key[None, :], (8, ROWS)).astype(np.float32)
    sort = np.zeros((QUAD, QUAD), np.float32)
    for j in range(4):
        for c in range(NCH):
            for slot in range(CAP):
                sort[c * 48 + j * CAP + slot, j * MSG + c * CAP + slot] = 1.0
    before = np.triu(np.ones((TOK, TOK), np.float32), 1)
    return key_col, key_row, sort, sort.T.copy(), before


def _kernel(
    held,
    fresh,
    ids_held,
    ids_fresh,
    routes,
    attn_gain,
    query_gain,
    key_gain,
    ffn_gain,
    router,
    w_in_hbm,
    w_out_hbm,
    key_col,
    key_row,
    sort,
    unsort,
    before,
    out_hbm,
    w_part,
    w_in,
    w_out,
    recv_d,
    recv_c,
    send_d,
    send_c,
    rows_in,
    inner,
    staged,
    pick,
    comb,
    cur,
    normed,
    far,
    prior,
    res,
    moe,
    out_half,
    sums,
    stat_send,
    stat_recv,
    row_send,
    row_recv,
    columns,
    ids_own,
    ids_pri,
    s_w,
    s_ids_send,
    s_ids_recv,
    s_prior_send,
    s_prior_recv,
    s_stat_send,
    s_stat_recv,
    s_carry,
    s_row_send,
    s_row_recv,
    s_d_send,
    s_d_recv,
    s_c_send,
    s_c_recv,
    s_out,
    s_out_send,
    s_out_recv,
):
    s = lax.axis_index("section")
    e = lax.axis_index("expert")
    h = lax.axis_index("dp")
    z, y, xl = e // 8, (e // 2) % 4, e % 2
    x = h * 2 + xl
    start_col = pl.multiple_of(h * HALF, HALF)

    def at(section, expert, dp):
        return {"section": section, "expert": expert, "dp": dp}

    def offset(j):
        k = (13 * j) % 32
        return k % 2, (k // 2) % 4, k // 8

    def ahead(m):
        dx, dy, dz = offset(m // 2)
        x2 = (x + dx + 2 * (m % 2)) % 4
        return ((z + dz) % 4) * 8 + ((y + dy) % 4) * 2 + x2 % 2, x2 // 2

    def behind(j):
        dx, dy, dz = offset(j)
        return ((z + 4 - dz) % 4) * 8 + ((y + 4 - dy) % 4) * 2 + (xl + dx) % 2

    nxt, prv = (e + 1) % EXP, (e + EXP - 1) % EXP

    load_out = pltpu.make_async_copy(w_out_hbm, w_out, s_w.at[2])
    load_out.start()

    def load_in(i):
        return pltpu.make_async_copy(
            w_in_hbm.at[pl.ds(i * WROWS, WROWS)], w_part.at[i % 2], s_w.at[i % 2]
        )

    load_in(0).start()
    load_in(1).start()

    barrier = pltpu.get_barrier_semaphore()

    @pl.loop(1, 2 * EXP)
    def _(m):
        e2, h2 = ahead(m)
        pl.semaphore_signal(barrier, inc=1, device_id=at(s, e2, h2), device_id_type=MESH)

    for e2, h2 in ((e, h), (e, 1 - h), (nxt, h), (prv, h)):
        pl.semaphore_signal(barrier, inc=1, device_id=at(1 - s, e2, h2), device_id_type=MESH)

    ids_own[0] = jnp.broadcast_to(ids_held[...], (8, TOK))

    @pl.when(s == 0)
    def _():
        ids_own[1] = jnp.broadcast_to(ids_fresh[...], (8, TOK))

    def send_ids(src, dst, i, j, device):
        return pltpu.make_async_remote_copy(
            src_ref=src,
            dst_ref=dst,
            send_sem=s_ids_send.at[i],
            recv_sem=s_ids_recv.at[j],
            device_id=device,
            device_id_type=MESH,
        )

    ids_0 = send_ids(ids_own.at[0], ids_pri.at[0], 0, 0, at(s, nxt, h))
    ids_1 = send_ids(ids_own.at[1], ids_pri.at[1], 1, 1, at(0, nxt, h))
    ids_2 = send_ids(ids_own.at[0], ids_own.at[1], 2, 2, at(1, e, h))
    ids_3 = send_ids(ids_own.at[0], ids_pri.at[1], 3, 1, at(1, nxt, h))
    def head_cols(c):
        return pl.ds(pl.multiple_of(c * TOK, TOK), TOK)

    def own_cols(c):
        return pl.ds(pl.multiple_of(start_col + c * TOK, TOK), TOK)

    def take_input(ref, t):
        def add(i, total):
            for j in range(8):
                wide = ref[:, head_cols(i * 8 + j)].astype(F32)
                total = total + wide * wide
            return total

        total = lax.fori_loop(0, D // TOK // 8, add, jnp.zeros((TOK, TOK), F32))
        scale = lax.rsqrt(jnp.sum(total, axis=1, keepdims=True) * (1.0 / D) + EPS)
        cur[t] = ref[:, pl.ds(start_col, HALF)]
        far_col = pl.multiple_of((1 - h) * HALF + HALF // 2, HALF // 2)

        @pl.loop(0, 2)
        def _(i):
            for j in range(4):
                c = i * 4 + j
                cols = pl.ds(pl.multiple_of(far_col + c * TOK, TOK), TOK)
                wide = ref[:, cols].astype(F32)
                gain = attn_gain[:, cols].astype(F32)
                far[t, :, head_cols(c)] = (wide * scale * gain).astype(BF)

        norm(t, scale)
        prior_copy(t, 0, 0).start()
        prior_copy(t, 1, 1).start()

    def norm(t, scale):
        @pl.loop(0, HALF // TOK, unroll=4)
        def _(c):
            wide = cur[t, :, head_cols(c)].astype(F32)
            gain = attn_gain[:, own_cols(c)].astype(F32)
            normed[t, :, head_cols(c)] = (wide * scale * gain).astype(BF)

    def prior_copy(t, piece, across):
        cols = pl.ds(piece * (HALF // 2), HALF // 2)
        return pltpu.make_async_remote_copy(
            src_ref=far.at[t] if across else normed.at[t, :, cols],
            dst_ref=prior.at[t, :, cols],
            send_sem=s_prior_send.at[t, piece],
            recv_sem=s_prior_recv.at[t, piece],
            device_id=at(s, nxt, 1 - h if across else h),
            device_id_type=MESH,
        )

    def carry_copy():
        return pltpu.make_async_remote_copy(
            src_ref=out_half.at[0],
            dst_ref=cur.at[1],
            send_sem=s_carry.at[0],
            recv_sem=s_carry.at[1],
            device_id=at(1, e, h),
            device_id_type=MESH,
        )

    def row_copy(i):
        return pltpu.make_async_remote_copy(
            src_ref=row_send,
            dst_ref=row_recv.at[h],
            send_sem=s_row_send.at[i],
            recv_sem=s_row_recv.at[h],
            device_id=at(1, e, (h + i) % 2),
            device_id_type=MESH,
        )

    def stat_copy(t):
        return pltpu.make_async_remote_copy(
            src_ref=stat_send.at[t],
            dst_ref=stat_recv.at[t],
            send_sem=s_stat_send.at[t],
            recv_sem=s_stat_recv.at[t],
            device_id=at(s, e, 1 - h),
            device_id_type=MESH,
        )

    pl.semaphore_wait(barrier, 2 * EXP - 1 + 4)
    take_input(held, 0)
    ids_0.start()

    @pl.when(s == 0)
    def _():
        ids_1.start()
        ids_2.start()
        ids_3.start()
        take_input(fresh, 1)

    def send_dispatch(t):
        @pl.loop(1, 2 * EXP)
        def _(m):
            e2, h2 = ahead(m)
            j = m // 2
            pltpu.make_async_remote_copy(
                src_ref=send_d.at[t, pl.ds(pl.multiple_of(e2 * MSG, MSG), MSG)],
                dst_ref=recv_d.at[t, j // 4, h, pl.ds(pl.multiple_of((j % 4) * MSG, MSG), MSG)],
                send_sem=s_d_send.at[t, m],
                recv_sem=s_d_recv.at[t, j // 4],
                device_id=at(s, e2, h2),
                device_id_type=MESH,
            ).start()

        pltpu.make_async_copy(
            send_d.at[t, pl.ds(pl.multiple_of(e * MSG, MSG), MSG)],
            recv_d.at[t, 0, h, pl.ds(0, MSG)],
            s_d_recv.at[t, 0],
        ).start()
    def attention_stage(t):
        @pl.when((t == 1) & (s == 1))
        def _():
            carry_copy().wait_recv()
            for i in range(2):
                pltpu.make_async_remote_copy(
                    src_ref=row_send,
                    dst_ref=row_recv.at[i],
                    send_sem=s_row_send.at[i],
                    recv_sem=s_row_recv.at[i],
                    device_id=at(1, e, h),
                    device_id_type=MESH,
                ).wait_recv()
            total = row_recv[0] + row_recv[1]
            norm(1, lax.rsqrt(jnp.sum(total, axis=1, keepdims=True) * (1.0 / D) + EPS))
            prior_copy(1, 0, 0).start()
            prior_copy(1, 1, 0).start()
            ids_2.wait_recv()

        chosen = routes[t]
        label = lax.broadcasted_iota(jnp.int32, (EXP, TOK), 0)
        first = (label == chosen[0:1]).astype(F32)
        second = (label == chosen[1:2]).astype(F32)
        ranking = jnp.dot((first + second).astype(BF), before[...], preferred_element_type=F32)
        place_0 = jnp.sum((ranking + label.astype(F32) * CAP) * first, axis=0, keepdims=True)
        place_1 = jnp.sum((ranking + label.astype(F32) * CAP) * second, axis=0, keepdims=True)

        @pl.loop(0, ROWS // TOK)
        def _(r):
            rows = pl.ds(pl.multiple_of(r * TOK, TOK), TOK)
            keys = key_col[rows, :]
            for c in range(NCH):
                hit = (keys == place_0 + 1024.0 * c) | (keys == place_1 + 1024.0 * c)
                pick[rows, c * TOK : (c + 1) * TOK] = hit.astype(F32).astype(BF)

        @pl.when(t == 0)
        def _():
            ids_0.wait_recv()

        @pl.when(t == 1)
        def _():
            ids_1.wait_recv()

        row_ids = jnp.broadcast_to(ids_own[t, 0:1, :].astype(F32), (TOK, TOK))
        prior_ids = jnp.broadcast_to(ids_pri[t, 0:1, :].astype(F32), (TOK, TOK))
        col_ids = jnp.transpose(row_ids)
        causal = lax.broadcasted_iota(jnp.int32, (TOK, TOK), 1) <= lax.broadcasted_iota(
            jnp.int32, (TOK, TOK), 0
        )
        own_mask = jnp.where((col_ids == row_ids) & causal, 0.0, -1e30)
        pri_mask = jnp.where((col_ids == prior_ids) & (e > 0), 0.0, -1e30)
        sums[...] = jnp.zeros((TOK, TOK), F32)

        @pl.loop(0, NCH)
        def _(quad):
            @pl.when(quad == 0)
            def _():
                prior_copy(t, 0, 0).wait_recv()

            @pl.when(quad == 2)
            def _():
                prior_copy(t, 1, 0).wait_recv()

            rows = pl.ds(pl.multiple_of(quad * TOK, TOK), TOK)
            for i in range(4):
                c = quad * 4 + i
                own = normed[t, :, head_cols(c)]
                pri = prior[t, :, head_cols(c)]
                q_gain = query_gain[:, own_cols(c)].astype(F32)
                k_gain = key_gain[:, own_cols(c)].astype(F32)
                queries = (own.astype(F32) * q_gain).astype(BF)
                own_keys = (own.astype(F32) * k_gain).astype(BF)
                pri_keys = (pri.astype(F32) * k_gain).astype(BF)
                dims = (((1,), (1,)), ((), ()))
                own_s = lax.dot_general(queries, own_keys, dims, preferred_element_type=F32)
                pri_s = lax.dot_general(queries, pri_keys, dims, preferred_element_type=F32)
                own_s = own_s * TOK**-0.5 + own_mask
                pri_s = pri_s * TOK**-0.5 + pri_mask
                top = jnp.max(jnp.maximum(own_s, pri_s), axis=1, keepdims=True)
                own_p = jnp.exp(own_s - top)
                pri_p = jnp.exp(pri_s - top)
                total = jnp.sum(own_p + pri_p, axis=1, keepdims=True)
                share = 1.0 / total
                mixed = jnp.dot((own_p * share).astype(BF), own, preferred_element_type=F32)
                mixed += jnp.dot((pri_p * share).astype(BF), pri, preferred_element_type=F32)
                summed = cur[t, :, head_cols(c)].astype(F32) + mixed.astype(BF).astype(F32)
                res[t, :, head_cols(c)] = summed
                sums[...] += summed * summed
                f_gain = ffn_gain[:, own_cols(c)].astype(F32)
                moe[rows, i * TOK : (i + 1) * TOK] = (summed * f_gain).astype(BF)

        stat_send[t, 0:TOK, :] = sums[...]
        part = jnp.zeros((EXP, TOK), F32)
        for c in range(NCH):
            part += lax.dot_general(
                router[:, pl.ds(pl.multiple_of(start_col + c * CH, CH), CH)],
                moe[c * TOK : (c + 1) * TOK, :],
                (((1,), (1,)), ((), ())),
                preferred_element_type=F32,
            )
        stat_send[t, TOK:, :] = part
        stat_copy(t).start()
        stat_copy(t).wait_recv()
        sums[...] = stat_send[t, 0:TOK, :] + stat_recv[t, 0:TOK, :]
        logits = stat_send[t, TOK:, :] + stat_recv[t, TOK:, :]
        scale = lax.rsqrt(jnp.sum(sums[...], axis=1, keepdims=True) * (1.0 / D) + EPS)

        @pl.loop(0, NCH)
        def _(quad):
            rows = pl.ds(pl.multiple_of(quad * TOK, TOK), TOK)
            for i in range(4):
                c = quad * 4 + i
                f_gain = ffn_gain[:, own_cols(c)].astype(F32)
                moe[rows, i * TOK : (i + 1) * TOK] = (
                    res[t, :, head_cols(c)] * scale * f_gain
                ).astype(BF)

        @pl.loop(0, EXP // 4)
        def _(g):
            rows = pl.ds(pl.multiple_of(g * QUAD, QUAD), QUAD)
            send_d[t, rows, :] = jnp.dot(
                pick[rows, :], moe[...], preferred_element_type=F32
            ).astype(BF)

        send_dispatch(t)

        scale_row = jnp.transpose(jnp.broadcast_to(scale, (TOK, TOK)))
        logits = logits * scale_row[0:EXP, :]
        logit_0 = jnp.sum(logits * first, axis=0, keepdims=True)
        logit_1 = jnp.sum(logits * second, axis=0, keepdims=True)
        top = jnp.maximum(logit_0, logit_1)
        raised_0, raised_1 = jnp.exp(logit_0 - top), jnp.exp(logit_1 - top)

        def column(row):
            return jnp.transpose(jnp.broadcast_to(row, (TOK, TOK)))

        columns[t, 0] = column(raised_0 / (raised_0 + raised_1))
        columns[t, 1] = column(raised_1 / (raised_0 + raised_1))
        columns[t, 2] = column(place_0)
        columns[t, 3] = column(place_1)

        @pl.when(t == 0)
        def _():
            @pl.loop(0, D // WROWS)
            def _(i):
                load_in(i).wait()
                rows = pl.ds(pl.multiple_of(i * WROWS, WROWS), WROWS)
                w_in[rows, :] = w_part[i % 2].reshape(WROWS, 2 * HID)

                @pl.when(i + 2 < D // WROWS)
                def _():
                    load_in(i + 2).start()

            load_out.wait()

    def expert_stage(t):
        @pl.loop(0, 2)
        def _(block):
            @pl.loop(0, 4)
            def _(i):
                g = block * 4 + i
                pltpu.make_async_copy(
                    recv_d.at[t, g], recv_d.at[t, g], s_d_recv.at[t, g]
                ).wait()
                for p in range(2):
                    sorted_rows = jnp.dot(
                        sort[...], recv_d[t, g, p], preferred_element_type=F32
                    ).astype(BF)
                    for c in range(NCH):
                        rows_in[
                            pl.ds(pl.multiple_of(i * 48, 48), 48),
                            p * HALF + c * CH : p * HALF + (c + 1) * CH,
                        ] = sorted_rows[c * 48 : (c + 1) * 48]

            @pl.loop(0, HID // 256)
            def _(n):
                gate = jnp.dot(
                    rows_in[...],
                    w_in[:, pl.ds(pl.multiple_of(n * 256, 256), 256)],
                    preferred_element_type=F32,
                )
                up = jnp.dot(
                    rows_in[...],
                    w_in[:, pl.ds(pl.multiple_of(HID + n * 256, 256), 256)],
                    preferred_element_type=F32,
                )
                inner[:, pl.ds(pl.multiple_of(n * 256, 256), 256)] = (
                    gate / (1.0 + jnp.exp(-gate)) * up
                ).astype(BF)

            @pl.loop(0, 2)
            def _(p):
                for c in range(NCH):
                    col = pl.multiple_of(p * HALF + c * CH, CH)
                    staged[c] = jnp.dot(
                        inner[...], w_out[:, pl.ds(col, CH)], preferred_element_type=F32
                    ).astype(BF)

                @pl.loop(0, 4)
                def _(i):
                    g = block * 4 + i
                    rows = pl.ds(pl.multiple_of(i * 48, 48), 48)
                    stack = staged[:, rows, :].reshape(QUAD, CH)
                    packed = jnp.dot(unsort[...], stack, preferred_element_type=F32)
                    send_c[t, p, pl.ds(pl.multiple_of(g * QUAD, QUAD), QUAD), :] = packed.astype(BF)

                    @pl.when((s == 1) | (t == 0))
                    def _():
                        send_results(t, p, g)

    def send_results(t, p, g):
        @pl.loop(0, 4)
        def _(i):
            j = g * 4 + i
            remote = (j > 0) | (p != h)
            src = send_c.at[t, p, pl.ds(pl.multiple_of(j * MSG, MSG), MSG)]
            dst = recv_c.at[t, h, pl.ds(pl.multiple_of(e * MSG, MSG), MSG)]

            @pl.when(remote)
            def _():
                m = jnp.where(j > 0, j * 2 + p, 1)
                pltpu.make_async_remote_copy(
                    src_ref=src,
                    dst_ref=dst,
                    send_sem=s_c_send.at[t, m],
                    recv_sem=s_c_recv.at[t],
                    device_id=at(s, behind(j), p),
                    device_id_type=MESH,
                ).start()

            @pl.when(jnp.logical_not(remote))
            def _():
                pltpu.make_async_copy(src, dst, s_c_recv.at[t]).start()

    def combine_stage(t):
        @pl.loop(0, ROWS // TOK)
        def _(r):
            cols = pl.ds(pl.multiple_of(r * TOK, TOK), TOK)
            keys = key_row[0:1, cols]
            for c in range(NCH):
                value = jnp.where(keys == columns[t, 2] + 1024.0 * c, columns[t, 0], 0.0)
                value += jnp.where(keys == columns[t, 3] + 1024.0 * c, columns[t, 1], 0.0)
                comb[c, :, cols] = value.astype(BF)

        pltpu.make_async_copy(recv_c.at[t], recv_c.at[t], s_c_recv.at[t]).wait()
        total = jnp.zeros((TOK, TOK), F32)
        for c in range(NCH):
            combined = jnp.dot(comb[c], recv_c[t, 0], preferred_element_type=F32)
            combined += jnp.dot(comb[c], recv_c[t, 1], preferred_element_type=F32)
            final = (res[t, :, c * CH : (c + 1) * CH] + combined).astype(BF)
            out_half[t, :, c * CH : (c + 1) * CH] = final
            for i in range(CH // TOK):
                wide = final[:, i * TOK : (i + 1) * TOK].astype(F32)
                total = total + wide * wide

            @pl.when(t == 1)
            def _():
                far_out(1, c).start()

        @pl.when((t == 0) & (s == 0))
        def _():
            carry_copy().start()
            row_send[...] = total
            for i in range(2):
                row_copy(i).start()

            @pl.loop(0, 2)
            def _(p):
                @pl.loop(0, EXP // 4)
                def _(g):
                    send_results(1, p, g)

        @pl.when(t == 0)
        def _():
            for c in range(NCH):
                far_out(0, c).start()

        near_out(t).start()

    def near_out(t):
        return pltpu.make_async_copy(
            out_half.at[t], out_hbm.at[t, :, pl.ds(start_col, HALF)], s_out.at[t]
        )

    def far_out(t, c):
        return pltpu.make_async_remote_copy(
            src_ref=out_half.at[t, :, pl.ds(c * CH, CH)],
            dst_ref=out_hbm.at[t, :, pl.ds(pl.multiple_of(start_col + c * CH, CH), CH)],
            send_sem=s_out_send.at[t, c],
            recv_sem=s_out_recv.at[t, c],
            device_id=at(s, e, 1 - h),
            device_id_type=MESH,
        )

    @pl.loop(0, 6)
    def _(step):
        @pl.when((step == 0) | (step == 1 + s))
        def _():
            attention_stage((step + 1) // 2)

        @pl.when((step == 2 - s) | (step == 3 + s))
        def _():
            expert_stage(step // 3)

        @pl.when((step == 4 - s) | (step == 5))
        def _():
            combine_stage(step // 5)

    @pl.loop(0, 2)
    def _(t):
        near_out(t).wait()
        for c in range(NCH):
            far_out(t, c).wait()
        prior_copy(t, 0, 0).wait_send()
        prior_copy(t, 1, 0).wait_send()
        stat_copy(t).wait_send()

    @pl.loop(1, 2 * EXP)
    def _(m):
        for t in range(2):
            pltpu.make_async_remote_copy(
                src_ref=send_c.at[0, 0, pl.ds(0, MSG)],
                dst_ref=recv_c.at[0, 0, pl.ds(0, MSG)],
                send_sem=s_c_send.at[t, m],
                recv_sem=s_c_recv.at[0],
                device_id=at(s, nxt, h),
                device_id_type=MESH,
            ).wait_send()
            pltpu.make_async_remote_copy(
                src_ref=send_d.at[0, pl.ds(0, MSG)],
                dst_ref=recv_d.at[0, 0, 0, pl.ds(0, MSG)],
                send_sem=s_d_send.at[t, m],
                recv_sem=s_d_recv.at[0, 0],
                device_id=at(s, nxt, h),
                device_id_type=MESH,
            ).wait_send()

    ids_0.wait_send()

    @pl.when(s == 0)
    def _():
        ids_1.wait_send()
        ids_2.wait_send()
        ids_3.wait_send()
        carry_copy().wait_send()
        for i in range(2):
            row_copy(i).wait_send()


def body(
    hidden_held,
    fresh_rows,
    doc_held,
    doc_fresh,
    routes,
    attn_gain,
    query_gain,
    key_gain,
    ffn_gain,
    router,
    weight_in,
    weight_out,
):
    key_col, key_row, sort, unsort, before = _constants()
    vmem = pl.BlockSpec(memory_space=pltpu.VMEM)
    hbm = pl.BlockSpec(memory_space=pl.ANY)
    dma = pltpu.SemaphoreType.DMA
    out = pl.pallas_call(
        _kernel,
        out_shape=jax.ShapeDtypeStruct((2, TOK, D), BF),
        in_specs=[vmem] * 10 + [hbm] * 2 + [vmem] * 5,
        out_specs=hbm,
        scratch_shapes=[
            pltpu.VMEM((2, WROWS, 2, HID), BF),
            pltpu.VMEM((D, 2 * HID), BF),
            pltpu.VMEM((HID, D), BF),
            pltpu.VMEM((2, EXP // 4, 2, QUAD, CH), BF),
            pltpu.VMEM((2, 2, ROWS, CH), BF),
            pltpu.VMEM((2, ROWS, CH), BF),
            pltpu.VMEM((2, 2, ROWS, CH), BF),
            pltpu.VMEM((SLOTS // 2, D), BF),
            pltpu.VMEM((SLOTS // 2, HID), BF),
            pltpu.VMEM((NCH, SLOTS // 2, CH), BF),
            pltpu.VMEM((ROWS, NCH * TOK), BF),
            pltpu.VMEM((NCH, TOK, ROWS), BF),
            pltpu.VMEM((2, TOK, HALF), BF),
            pltpu.VMEM((2, TOK, HALF), BF),
            pltpu.VMEM((2, TOK, HALF // 2), BF),
            pltpu.VMEM((2, TOK, HALF), BF),
            pltpu.VMEM((2, TOK, HALF), F32),
            pltpu.VMEM((NCH * TOK, CH), BF),
            pltpu.VMEM((2, TOK, HALF), BF),
            pltpu.VMEM((TOK, TOK), F32),
            pltpu.VMEM((2, TOK + EXP, TOK), F32),
            pltpu.VMEM((2, TOK + EXP, TOK), F32),
            pltpu.VMEM((TOK, TOK), F32),
            pltpu.VMEM((2, TOK, TOK), F32),
            pltpu.VMEM((2, 4, TOK, TOK), F32),
            pltpu.VMEM((2, 8, TOK), jnp.int32),
            pltpu.VMEM((2, 8, TOK), jnp.int32),
            dma((3,)),
            dma((4,)),
            dma((3,)),
            dma((2, 2)),
            dma((2, 2)),
            dma((2,)),
            dma((2,)),
            dma((2,)),
            dma((2,)),
            dma((2,)),
            dma((2, 2 * EXP)),
            dma((2, EXP // 4)),
            dma((2, 2 * EXP)),
            dma((2,)),
            dma((2,)),
            dma((2, NCH)),
            dma((2, NCH)),
        ],
        compiler_params=pltpu.CompilerParams(
            collective_id=0, has_side_effects=True, vmem_limit_bytes=62 << 20
        ),
        cost_estimate=pl.CostEstimate(
            flops=25_000_000_000, bytes_accessed=25_000_000, transcendentals=5_000_000
        ),
    )(
        hidden_held[0],
        fresh_rows[0],
        doc_held,
        doc_fresh,
        jnp.swapaxes(routes[:, 0], 1, 2),
        attn_gain,
        query_gain,
        key_gain,
        ffn_gain,
        router[0].T,
        weight_in[0, 0],
        weight_out[0, 0],
        jnp.asarray(key_col),
        jnp.asarray(key_row),
        jnp.asarray(sort, BF),
        jnp.asarray(unsort, BF),
        jnp.asarray(before, BF),
    )
    return out[:, None]


def solution(mesh):
    in_specs = (
        P("section", "expert", None),
        P(None, "expert", None),
        P("section", "expert"),
        P(None, "expert"),
        P(None, "section", "expert", None),
        P("section", None),
        P("section", None),
        P("section", None),
        P("section", None),
        P("section", None, None),
        P("section", "expert", None, None, "dp"),
        P("section", "expert", "dp", None),
    )
    out_specs = P(None, "section", "expert", None)
    return jax.shard_map(body, mesh=mesh, in_specs=in_specs, out_specs=out_specs, check_vma=False)
```

time: 299 us -> 246 us (0.82)
  Pallas kernels: 280 us -> 242 us
  local copies, waits for them, and re-layouts: 16.2 us -> 3.13 us
    pallas_call x1, Pallas kernels: 280 us -> 242 us  [body(): pl.pallas_call(_kernel, out_shape=jax.ShapeDtypeStruct((2, TOK, D), BF),...]
    unnamed x2 -> x1, local copies, waits for them, and re-layouts: 16.2 us -> 3.13 us
where the time goes in v2:
time: 246 us; the launch traced here: 245 us
  Pallas kernels  242 us (98%)
  local copies, waits for them, and re-layouts  3.13 us (1%)
    pallas_call x1, Pallas kernels, body(): pl.pallas_call(_kernel, out_shape=jax.ShapeDtypeStruct((2, TOK, D), BF),...  242 us

profile of v2, /device:TPU:3, one launch (start us, length us, event | category | flops | bytes accessed | tf_op | source)
XLA Modules:
  0.0 245.4 jit_solution(14618592805865911521)
XLA Ops:
  0.0 242.2 %shard_map.163 = bf16[2,128,4096]{2,1,0:T(8,128)(2,1)} custom-call(bf16[128,4096]{1,0:T(8,128)(2,1)} %bitcast.16, bf16[128,4096]{1,0:T(8,128)(2,1)} %bitcast.17, s32[1,128]{1,0:T(1,128)} %ids_held.1, s32[1,128]{1,0:T(1,128)} %ids_fresh.1, s32[2,2,128]{2,1,0:T(2,128)} %bitcast.19, bf16[1,4096]{1,0:T(2,128)(2,1)} %attn_gain.1, bf16[1,4096]{1,0:T(2,128)(2,1)} %query_gain.1, ...), custom_call_target="tpu_custom_call" | custom-call | flops 24999999488 | bytes 25000000 | tf_op jit(solution)/shard_map/pallas_call | solution.py:649
  242.2 3.1 %copy.20 = bf16[2,1,128,4096]{3,2,1,0:T(8,128)(2,1)} copy(bf16[2,1,128,4096]{3,2,1,0:T(8,128)(2,1)} %bitcast.13) | data formatting | bytes 4194304

commit v3 on v2

--- a/solution.py
+++ b/solution.py
@@ -41,8 +41,8 @@
 
 
 def _kernel(
-    held,
-    fresh,
+    held_hbm,
+    fresh_hbm,
     ids_held,
     ids_fresh,
     routes,
@@ -53,12 +53,15 @@
     router,
     w_in_hbm,
     w_out_hbm,
-    key_col,
+    key_col_hbm,
     key_row,
     sort,
     unsort,
     before,
     out_hbm,
+    held,
+    fresh,
+    key_col,
     w_part,
     w_in,
     w_out,
@@ -87,6 +90,7 @@
     ids_own,
     ids_pri,
     s_w,
+    s_in,
     s_ids_send,
     s_ids_recv,
     s_prior_send,
@@ -103,6 +107,7 @@
     s_out,
     s_out_send,
     s_out_recv,
+    s_here,
 ):
     s = lax.axis_index("section")
     e = lax.axis_index("expert")
@@ -129,6 +134,34 @@
 
     nxt, prv = (e + 1) % EXP, (e + EXP - 1) % EXP
 
+    load_held = pltpu.make_async_copy(held_hbm, held, s_in.at[0])
+    load_fresh = pltpu.make_async_copy(fresh_hbm, fresh, s_in.at[1])
+    load_keys = pltpu.make_async_copy(key_col_hbm, key_col, s_in.at[2])
+    load_held.start()
+    barrier = pltpu.get_barrier_semaphore()
+
+    def along(axis, i):
+        if axis == 0:
+            x2 = (x + i) % 4
+            return at(s, e - xl + x2 % 2, x2 // 2)
+        if axis == 1:
+            return at(s, z * 8 + ((y + i) % 4) * 2 + xl, h)
+        return at(s, ((z + i) % 4) * 8 + y * 2 + xl, h)
+
+    def greet(axis, sem):
+        for i in range(1, 4):
+            pl.semaphore_signal(sem, inc=1, device_id=along(axis, i), device_id_type=MESH)
+
+    for e2 in (nxt, prv):
+        for h2 in (h, 1 - h):
+            pl.semaphore_signal(barrier, inc=1, device_id=at(s, e2, h2), device_id_type=MESH)
+    for e2, h2 in ((e, h), (e, 1 - h), (nxt, h), (prv, h)):
+        pl.semaphore_signal(barrier, inc=1, device_id=at(1 - s, e2, h2), device_id_type=MESH)
+    for axis in range(3):
+        greet(axis, barrier)
+
+    load_keys.start()
+    load_fresh.start()
     load_out = pltpu.make_async_copy(w_out_hbm, w_out, s_w.at[2])
     load_out.start()
 
@@ -139,16 +172,6 @@
 
     load_in(0).start()
     load_in(1).start()
-
-    barrier = pltpu.get_barrier_semaphore()
-
-    @pl.loop(1, 2 * EXP)
-    def _(m):
-        e2, h2 = ahead(m)
-        pl.semaphore_signal(barrier, inc=1, device_id=at(s, e2, h2), device_id_type=MESH)
-
-    for e2, h2 in ((e, h), (e, 1 - h), (nxt, h), (prv, h)):
-        pl.semaphore_signal(barrier, inc=1, device_id=at(1 - s, e2, h2), device_id_type=MESH)
 
     ids_own[0] = jnp.broadcast_to(ids_held[...], (8, TOK))
 
@@ -188,30 +211,32 @@
         cur[t] = ref[:, pl.ds(start_col, HALF)]
         far_col = pl.multiple_of((1 - h) * HALF + HALF // 2, HALF // 2)
 
-        @pl.loop(0, 2)
-        def _(i):
+        norm(t, scale, 2)
+        for piece in range(2):
             for j in range(4):
-                c = i * 4 + j
+                c = piece * 4 + j
                 cols = pl.ds(pl.multiple_of(far_col + c * TOK, TOK), TOK)
                 wide = ref[:, cols].astype(F32)
                 gain = attn_gain[:, cols].astype(F32)
                 far[t, :, head_cols(c)] = (wide * scale * gain).astype(BF)
-
-        norm(t, scale)
-        prior_copy(t, 0, 0).start()
-        prior_copy(t, 1, 1).start()
-
-    def norm(t, scale):
-        @pl.loop(0, HALF // TOK, unroll=4)
-        def _(c):
-            wide = cur[t, :, head_cols(c)].astype(F32)
-            gain = attn_gain[:, own_cols(c)].astype(F32)
-            normed[t, :, head_cols(c)] = (wide * scale * gain).astype(BF)
+            prior_copy(t, 2 + piece, 1).start()
+
+    def norm(t, scale, sent):
+        for piece in range(NCH):
+            for i in range(4):
+                c = piece * 4 + i
+                wide = cur[t, :, head_cols(c)].astype(F32)
+                gain = attn_gain[:, own_cols(c)].astype(F32)
+                normed[t, :, head_cols(c)] = (wide * scale * gain).astype(BF)
+            if piece < sent:
+                prior_copy(t, piece, 0).start()
 
     def prior_copy(t, piece, across):
-        cols = pl.ds(piece * (HALF // 2), HALF // 2)
+        cols = pl.ds(piece * CH, CH)
         return pltpu.make_async_remote_copy(
-            src_ref=far.at[t] if across else normed.at[t, :, cols],
+            src_ref=far.at[t, :, pl.ds(piece * CH - HALF // 2, CH)]
+            if across
+            else normed.at[t, :, cols],
             dst_ref=prior.at[t, :, cols],
             send_sem=s_prior_send.at[t, piece],
             recv_sem=s_prior_recv.at[t, piece],
@@ -249,7 +274,9 @@
             device_id_type=MESH,
         )
 
-    pl.semaphore_wait(barrier, 2 * EXP - 1 + 4)
+    load_held.wait()
+    pl.semaphore_wait(barrier, 17)
+    greet(1, s_here.at[0])
     take_input(held, 0)
     ids_0.start()
 
@@ -258,7 +285,16 @@
         ids_1.start()
         ids_2.start()
         ids_3.start()
+        load_fresh.wait()
         take_input(fresh, 1)
+
+    @pl.when(s == 1)
+    def _():
+        load_fresh.wait()
+
+    load_keys.wait()
+    pl.semaphore_wait(s_here.at[0], 3)
+    greet(2, s_here.at[1])
 
     def send_dispatch(t):
         @pl.loop(1, 2 * EXP)
@@ -279,6 +315,19 @@
             recv_d.at[t, 0, h, pl.ds(0, MSG)],
             s_d_recv.at[t, 0],
         ).start()
+    def lay_out_weights():
+        @pl.loop(0, D // WROWS)
+        def _(i):
+            load_in(i).wait()
+            rows = pl.ds(pl.multiple_of(i * WROWS, WROWS), WROWS)
+            w_in[rows, :] = w_part[i % 2].reshape(WROWS, 2 * HID)
+
+            @pl.when(i + 2 < D // WROWS)
+            def _():
+                load_in(i + 2).start()
+
+        load_out.wait()
+
     def attention_stage(t):
         @pl.when((t == 1) & (s == 1))
         def _():
@@ -293,9 +342,7 @@
                     device_id_type=MESH,
                 ).wait_recv()
             total = row_recv[0] + row_recv[1]
-            norm(1, lax.rsqrt(jnp.sum(total, axis=1, keepdims=True) * (1.0 / D) + EPS))
-            prior_copy(1, 0, 0).start()
-            prior_copy(1, 1, 0).start()
+            norm(1, lax.rsqrt(jnp.sum(total, axis=1, keepdims=True) * (1.0 / D) + EPS), NCH)
             ids_2.wait_recv()
 
         chosen = routes[t]
@@ -334,13 +381,7 @@
 
         @pl.loop(0, NCH)
         def _(quad):
-            @pl.when(quad == 0)
-            def _():
-                prior_copy(t, 0, 0).wait_recv()
-
-            @pl.when(quad == 2)
-            def _():
-                prior_copy(t, 1, 0).wait_recv()
+            prior_copy(t, quad, 0).wait_recv()
 
             rows = pl.ds(pl.multiple_of(quad * TOK, TOK), TOK)
             for i in range(4):
@@ -403,7 +444,25 @@
                 pick[rows, :], moe[...], preferred_element_type=F32
             ).astype(BF)
 
-        send_dispatch(t)
+        @pl.when(t == 0)
+        def _():
+            pl.semaphore_wait(s_here.at[1], 3)
+
+        @pl.when((s == 1) & (t == 0))
+        def _():
+            lay_out_weights()
+
+        @pl.when((s == 1) | (t == 0))
+        def _():
+            send_dispatch(t)
+
+        @pl.when((s == 0) & (t == 0))
+        def _():
+            lay_out_weights()
+
+        @pl.when((s == 1) & (t == 1))
+        def _():
+            send_all_results(0)
 
         scale_row = jnp.transpose(jnp.broadcast_to(scale, (TOK, TOK)))
         logits = logits * scale_row[0:EXP, :]
@@ -419,20 +478,6 @@
         columns[t, 1] = column(raised_1 / (raised_0 + raised_1))
         columns[t, 2] = column(place_0)
         columns[t, 3] = column(place_1)
-
-        @pl.when(t == 0)
-        def _():
-            @pl.loop(0, D // WROWS)
-            def _(i):
-                load_in(i).wait()
-                rows = pl.ds(pl.multiple_of(i * WROWS, WROWS), WROWS)
-                w_in[rows, :] = w_part[i % 2].reshape(WROWS, 2 * HID)
-
-                @pl.when(i + 2 < D // WROWS)
-                def _():
-                    load_in(i + 2).start()
-
-            load_out.wait()
 
     def expert_stage(t):
         @pl.loop(0, 2)
@@ -485,9 +530,20 @@
                     packed = jnp.dot(unsort[...], stack, preferred_element_type=F32)
                     send_c[t, p, pl.ds(pl.multiple_of(g * QUAD, QUAD), QUAD), :] = packed.astype(BF)
 
-                    @pl.when((s == 1) | (t == 0))
+                    @pl.when((s == 0) | (t == 1))
                     def _():
                         send_results(t, p, g)
+
+        @pl.when((s == 0) & (t == 0))
+        def _():
+            send_dispatch(1)
+
+    def send_all_results(t):
+        @pl.loop(0, 2)
+        def _(p):
+            @pl.loop(0, EXP // 4)
+            def _(g):
+                send_results(t, p, g)
 
     def send_results(t, p, g):
         @pl.loop(0, 4)
@@ -545,12 +601,6 @@
             for i in range(2):
                 row_copy(i).start()
 
-            @pl.loop(0, 2)
-            def _(p):
-                @pl.loop(0, EXP // 4)
-                def _(g):
-                    send_results(1, p, g)
-
         @pl.when(t == 0)
         def _():
             for c in range(NCH):
@@ -579,11 +629,11 @@
         def _():
             attention_stage((step + 1) // 2)
 
-        @pl.when((step == 2 - s) | (step == 3 + s))
+        @pl.when((step == 2 - s) | (step == 4 - s))
         def _():
             expert_stage(step // 3)
 
-        @pl.when((step == 4 - s) | (step == 5))
+        @pl.when((step == 3 + s) | (step == 5))
         def _():
             combine_stage(step // 5)
 
@@ -592,8 +642,8 @@
         near_out(t).wait()
         for c in range(NCH):
             far_out(t, c).wait()
-        prior_copy(t, 0, 0).wait_send()
-        prior_copy(t, 1, 0).wait_send()
+        for piece in range(NCH):
+            prior_copy(t, piece, 0).wait_send()
         stat_copy(t).wait_send()
 
     @pl.loop(1, 2 * EXP)
@@ -649,9 +699,12 @@
     out = pl.pallas_call(
         _kernel,
         out_shape=jax.ShapeDtypeStruct((2, TOK, D), BF),
-        in_specs=[vmem] * 10 + [hbm] * 2 + [vmem] * 5,
+        in_specs=[hbm] * 2 + [vmem] * 8 + [hbm] * 3 + [vmem] * 4,
         out_specs=hbm,
         scratch_shapes=[
+            pltpu.VMEM((TOK, D), BF),
+            pltpu.VMEM((TOK, D), BF),
+            pltpu.VMEM((ROWS, TOK), F32),
             pltpu.VMEM((2, WROWS, 2, HID), BF),
             pltpu.VMEM((D, 2 * HID), BF),
             pltpu.VMEM((HID, D), BF),
@@ -680,10 +733,11 @@
             pltpu.VMEM((2, 8, TOK), jnp.int32),
             pltpu.VMEM((2, 8, TOK), jnp.int32),
             dma((3,)),
+            dma((3,)),
             dma((4,)),
             dma((3,)),
-            dma((2, 2)),
-            dma((2, 2)),
+            dma((2, NCH)),
+            dma((2, NCH)),
             dma((2,)),
             dma((2,)),
             dma((2,)),
@@ -696,6 +750,7 @@
             dma((2,)),
             dma((2, NCH)),
             dma((2, NCH)),
+            pltpu.SemaphoreType.REGULAR((2,)),
         ],
         compiler_params=pltpu.CompilerParams(
             collective_id=0, has_side_effects=True, vmem_limit_bytes=62 << 20

time: 246 us -> 229 us (0.931)
  the two profiles are of different devices: /device:TPU:3 before, /device:TPU:49 now
where the time goes in v3:
time: 229 us; the launch traced here: 228 us
  Pallas kernels  225 us (98%)
  local copies, waits for them, and re-layouts  3.13 us (1%)
    pallas_call x1, Pallas kernels, body(): pl.pallas_call(_kernel, out_shape=jax.ShapeDtypeStruct((2, TOK, D), BF),...  225 us

profile of v3, /device:TPU:49, one launch (start us, length us, event | category | flops | bytes accessed | tf_op | source)
XLA Modules:
  0.0 228.3 jit_solution(7775934135190888954)
XLA Ops:
  0.0 225.1 %shard_map.163 = bf16[2,128,4096]{2,1,0:T(8,128)(2,1)} custom-call(bf16[128,4096]{1,0:T(8,128)(2,1)} %bitcast.16, bf16[128,4096]{1,0:T(8,128)(2,1)} %bitcast.17, s32[1,128]{1,0:T(1,128)} %ids_held.1, s32[1,128]{1,0:T(1,128)} %ids_fresh.1, s32[2,2,128]{2,1,0:T(2,128)} %bitcast.19, bf16[1,4096]{1,0:T(2,128)(2,1)} %attn_gain.1, bf16[1,4096]{1,0:T(2,128)(2,1)} %query_gain.1, ...), custom_call_target="tpu_custom_call" | custom-call | flops 24999999488 | bytes 25000000 | tf_op jit(solution)/shard_map/pallas_call | solution.py:699
  225.1 3.1 %copy.20 = bf16[2,1,128,4096]{3,2,1,0:T(8,128)(2,1)} copy(bf16[2,1,128,4096]{3,2,1,0:T(8,128)(2,1)} %bitcast.13) | data formatting | bytes 4194304

commit v4 on v3

--- a/solution.py
+++ b/solution.py
@@ -274,9 +274,27 @@
             device_id_type=MESH,
         )
 
+    def lay_out_weights():
+        @pl.loop(0, D // WROWS)
+        def _(i):
+            load_in(i).wait()
+            rows = pl.ds(pl.multiple_of(i * WROWS, WROWS), WROWS)
+            w_in[rows, :] = w_part[i % 2].reshape(WROWS, 2 * HID)
+
+            @pl.when(i + 2 < D // WROWS)
+            def _():
+                load_in(i + 2).start()
+
+        load_out.wait()
+
     load_held.wait()
     pl.semaphore_wait(barrier, 17)
     greet(1, s_here.at[0])
+
+    @pl.when(s == 1)
+    def _():
+        lay_out_weights()
+
     take_input(held, 0)
     ids_0.start()
 
@@ -315,19 +333,6 @@
             recv_d.at[t, 0, h, pl.ds(0, MSG)],
             s_d_recv.at[t, 0],
         ).start()
-    def lay_out_weights():
-        @pl.loop(0, D // WROWS)
-        def _(i):
-            load_in(i).wait()
-            rows = pl.ds(pl.multiple_of(i * WROWS, WROWS), WROWS)
-            w_in[rows, :] = w_part[i % 2].reshape(WROWS, 2 * HID)
-
-            @pl.when(i + 2 < D // WROWS)
-            def _():
-                load_in(i + 2).start()
-
-        load_out.wait()
-
     def attention_stage(t):
         @pl.when((t == 1) & (s == 1))
         def _():
@@ -448,21 +453,13 @@
         def _():
             pl.semaphore_wait(s_here.at[1], 3)
 
-        @pl.when((s == 1) & (t == 0))
+        @pl.when((s == 1) | (t == 0))
+        def _():
+            send_dispatch(t)
+
+        @pl.when((s == 0) & (t == 0))
         def _():
             lay_out_weights()
-
-        @pl.when((s == 1) | (t == 0))
-        def _():
-            send_dispatch(t)
-
-        @pl.when((s == 0) & (t == 0))
-        def _():
-            lay_out_weights()
-
-        @pl.when((s == 1) & (t == 1))
-        def _():
-            send_all_results(0)
 
         scale_row = jnp.transpose(jnp.broadcast_to(scale, (TOK, TOK)))
         logits = logits * scale_row[0:EXP, :]
@@ -498,6 +495,10 @@
                             p * HALF + c * CH : p * HALF + (c + 1) * CH,
                         ] = sorted_rows[c * 48 : (c + 1) * 48]
 
+            @pl.when((s == 1) & (t == 1) & (block == 0))
+            def _():
+                send_all_results(0)
+
             @pl.loop(0, HID // 256)
             def _(n):
                 gate = jnp.dot(
@@ -538,6 +539,11 @@
         def _():
             send_dispatch(1)
 
+        @pl.when((s == 0) & (t == 1))
+        def _():
+            for c in range(NCH):
+                far_out(0, c).start()
+
     def send_all_results(t):
         @pl.loop(0, 2)
         def _(p):
@@ -601,7 +607,7 @@
             for i in range(2):
                 row_copy(i).start()
 
-        @pl.when(t == 0)
+        @pl.when((t == 0) & (s == 1))
         def _():
             for c in range(NCH):
                 far_out(0, c).start()

time: 229 us -> 230 us (level)
  the two profiles are of different devices: /device:TPU:49 before, /device:TPU:3 now
where the time goes in v4:
time: 230 us
  Pallas kernels  227 us (99%)
  local copies, waits for them, and re-layouts  3.13 us (1%)
    pallas_call x1, Pallas kernels, body(): pl.pallas_call(_kernel, out_shape=jax.ShapeDtypeStruct((2, TOK, D), BF),...  227 us

profile of v4, /device:TPU:3, one launch (start us, length us, event | category | flops | bytes accessed | tf_op | source)
XLA Modules:
  0.0 230.1 jit_solution(7650488081636242723)
XLA Ops:
  0.0 226.9 %shard_map.163 = bf16[2,128,4096]{2,1,0:T(8,128)(2,1)} custom-call(bf16[128,4096]{1,0:T(8,128)(2,1)} %bitcast.16, bf16[128,4096]{1,0:T(8,128)(2,1)} %bitcast.17, s32[1,128]{1,0:T(1,128)} %ids_held.1, s32[1,128]{1,0:T(1,128)} %ids_fresh.1, s32[2,2,128]{2,1,0:T(2,128)} %bitcast.19, bf16[1,4096]{1,0:T(2,128)(2,1)} %attn_gain.1, bf16[1,4096]{1,0:T(2,128)(2,1)} %query_gain.1, ...), custom_call_target="tpu_custom_call" | custom-call | flops 24999999488 | bytes 25000000 | tf_op jit(solution)/shard_map/pallas_call | solution.py:705
  226.9 3.1 %copy.20 = bf16[2,1,128,4096]{3,2,1,0:T(8,128)(2,1)} copy(bf16[2,1,128,4096]{3,2,1,0:T(8,128)(2,1)} %bitcast.13) | data formatting | bytes 4194304
